TPU v7x, 32 devices: a whole 2x2x4 slice. The times are simulated.
32 devices in a mesh: seq: 4 (over x, core), head: 8 (over z, y).
Axes of the slice: x: 2, y: 2, z: 4, core: 2. Of those that a mesh axis runs over, the one named last changes fastest.
Arguments:
- queries: float32 [1024, 512], P('seq', 'head'), may hold values from -50 to 50
- keys: float32 [1024, 512], P('seq', 'head'), may hold values from -16 to 16
- values: float32 [1024, 512], P('seq', 'head'), may hold values from -6 to 6
- local_span: int32 [4], replicated, may hold values from 1 to 2
- wo_local: float32 [512, 4096], P('head'), may hold values from -0.25 to 0.25
- wo_strided: float32 [512, 4096], P('head'), may hold values from -0.25 to 0.25
- grad_out: bfloat16 [1024, 4096], P('seq', 'head'), may hold values from -6 to 6
Outputs:
- mixed: float32 [1024, 4096], P('seq', 'head')
- grad_queries: float32 [1024, 512], P('seq', 'head')
- grad_keys: float32 [1024, 512], P('seq', 'head')
- grad_values: float32 [1024, 512], P('seq', 'head')
All inputs are finite; a program needn't handle non-finite values.
Results may differ from a plain program's by a relative error of at most 0.0003.
Values may be sent and summed in bfloat16 or wider, within the bound.
A program may use at most 64 MiB of HBM per device.

v0:
```python
import jax
import jax.numpy as jnp
from jax import lax
from jax.sharding import PartitionSpec as P

HDIM = 128
BLOCK = 128
GROUP_BLK = 2
STRIDE = 128


HIGHEST = lax.Precision.HIGHEST


def swapped(x, axis, distance):
    return lax.ppermute(x, axis, [(i, i ^ 1 << distance) for i in range(lax.axis_size(axis))])


def pair_sum(partial_value):
    return partial_value + swapped(partial_value, "head", 0)


def attend_forward(query_part, key_part, value_part, allowed):
    scale_factor = HDIM ** (-0.5)
    partial_value = jnp.einsum("bqhd,bkhd->bhqk", query_part, key_part, precision=HIGHEST)
    scores = pair_sum(partial_value) * scale_factor
    row_max = jnp.max(jnp.where(allowed, scores, -jnp.inf), axis=-1, keepdims=True)
    weights = jnp.where(allowed, jnp.exp(scores - row_max), 0.0)
    probs = weights / jnp.sum(weights, axis=-1, keepdims=True)
    attended = jnp.einsum("bhqk,bkhd->bqhd", probs, value_part, precision=HIGHEST)
    return (attended, probs)


def attend_backward(query_part, key_part, value_part, probs, attended, incoming):
    scale_factor = HDIM ** (-0.5)
    dprobs_part = jnp.einsum("bqhd,bkhd->bhqk", incoming, value_part, precision=HIGHEST)
    delta_part = jnp.transpose(jnp.sum(incoming * attended, axis=-1), (0, 2, 1))[..., None]
    joined = pair_sum(jnp.concatenate([dprobs_part, delta_part], axis=-1))
    dprobs = joined[..., :-1]
    row_delta = joined[..., -1:]
    dscores = probs * (dprobs - row_delta)
    grad_query = jnp.einsum("bhqk,bkhd->bqhd", dscores, key_part, precision=HIGHEST) * scale_factor
    grad_key = jnp.einsum("bhqk,bqhd->bkhd", dscores, query_part, precision=HIGHEST) * scale_factor
    grad_value = jnp.einsum("bhqk,bqhd->bkhd", probs, incoming, precision=HIGHEST)
    return (grad_query, grad_key, grad_value)


def to_strided(stacked):
    seq_devices = lax.axis_size("seq")
    tok_rows, members, head_dim = stacked.shape
    layout = stacked.reshape(tok_rows // seq_devices, seq_devices, members, head_dim)
    moved = lax.all_to_all(layout, "seq", split_axis=1, concat_axis=0, tiled=True)
    return moved.reshape(tok_rows, members, head_dim)


def to_contiguous(stacked):
    seq_devices = lax.axis_size("seq")
    tok_rows, members, head_dim = stacked.shape
    layout = stacked.reshape(seq_devices, tok_rows // seq_devices, 1, members, head_dim)
    moved = lax.all_to_all(layout, "seq", split_axis=0, concat_axis=2, tiled=True)
    return moved.reshape(tok_rows, members, head_dim)


def local(queries, keys, values, local_span, wo_local, wo_strided, grad_out):
    tok_rows, head_dim = queries.shape
    seq_devices = lax.axis_size("seq")
    per_run = STRIDE // seq_devices
    runs_here = tok_rows // per_run
    group_len = GROUP_BLK * BLOCK
    local_layout = (tok_rows // group_len, group_len, 1, head_dim)
    own_span = local_span[lax.axis_index("head") // 2]
    stacked = jnp.stack([queries, keys, values], axis=1)
    spread = to_strided(stacked)
    local_q = queries.reshape(local_layout)
    local_k = keys.reshape(local_layout)
    local_v = values.reshape(local_layout)
    position = jnp.arange(group_len)
    block_of = position // BLOCK
    causal = position[None, :] <= position[:, None]
    reach = block_of[:, None] - block_of[None, :] < own_span
    allowed_local = (causal & reach)[None, None]
    attn_local, probs_local = attend_forward(local_q, local_k, local_v, allowed_local)

    def to_runs(matrix):
        return matrix.reshape(runs_here, per_run, 1, head_dim).transpose(1, 0, 2, 3)

    def from_runs(arranged):
        return arranged.transpose(1, 0, 2, 3).reshape(tok_rows, head_dim)

    strided_q = to_runs(spread[:, 0])
    strided_k = to_runs(spread[:, 1])
    strided_v = to_runs(spread[:, 2])
    order = jnp.arange(runs_here)
    allowed_strided = (order[None, :] <= order[:, None])[None, None]
    attn_strided, probs_strided = attend_forward(strided_q, strided_k, strided_v, allowed_strided)
    strided_home = to_contiguous(from_runs(attn_strided)[:, None, :])[:, 0]
    attn_both = jnp.concatenate([attn_local.reshape(tok_rows, head_dim), strided_home], axis=1)
    wo_both = jnp.concatenate([wo_local, wo_strided], axis=0)
    w_cols = wo_both
    mixed_cols = lax.psum_scatter(
        lax.dot_general(
            w_cols,
            attn_both,
            (((0,), (1,)), ((), ())),
            precision=HIGHEST,
            preferred_element_type=jnp.float32,
        ),
        "head",
        scatter_dimension=0,
        tiled=True,
    )
    mixed = mixed_cols.T
    w_cols = wo_both
    grad_both = lax.dot_general(
        lax.all_gather(grad_out, "head", axis=1, tiled=True).astype(jnp.float32),
        w_cols,
        (((1,), (1,)), ((), ())),
        precision=HIGHEST,
        preferred_element_type=jnp.float32,
    )
    grad_local = grad_both[:, :head_dim]
    grad_strided = to_strided(grad_both[:, head_dim:][:, None, :])[:, 0]
    dq_local, dk_local, dv_local = attend_backward(
        local_q, local_k, local_v, probs_local, attn_local, grad_local.reshape(local_layout)
    )
    dq_strided, dk_strided, dv_strided = attend_backward(
        strided_q, strided_k, strided_v, probs_strided, attn_strided, to_runs(grad_strided)
    )
    strided_grads = jnp.stack(
        [from_runs(dq_strided), from_runs(dk_strided), from_runs(dv_strided)], axis=1
    )
    grads_home = to_contiguous(strided_grads)
    grad_queries = dq_local.reshape(tok_rows, head_dim) + grads_home[:, 0]
    grad_keys = dk_local.reshape(tok_rows, head_dim) + grads_home[:, 1]
    grad_values = dv_local.reshape(tok_rows, head_dim) + grads_home[:, 2]
    return (mixed, grad_queries, grad_keys, grad_values)


def solution(mesh):
    return jax.shard_map(
        local,
        mesh=mesh,
        in_specs=(
            P("seq", "head"),
            P("seq", "head"),
            P("seq", "head"),
            P(),
            P("head", None),
            P("head", None),
            P("seq", "head"),
        ),
        out_specs=(P("seq", "head"), P("seq", "head"), P("seq", "head"), P("seq", "head")),
        check_vma=False,
    )
```

profile of v0, /device:TPU:1, one launch (start us, length us, event | category | flops | bytes accessed | tf_op | source)
XLA Modules:
  0.0 190.3 jit_solution(5374624896689975967)
XLA Ops:
  11.8 4.3 %all-to-all-start = ((f32[4,1,12288]{2,1,0:T(1,128)}), f32[4,1,12288]{2,1,0:T(1,128)S(1)}, u32[]{:S(2)}, u32[]{:S(2)}) async-start(f32[4,1,12288]{2,1,0:T(1,128)} %reshape.266), calls=%async_computation | async-start | bytes 393216 | tf_op jit(solution)/shard_map/all_to_all | solution.py:52
  16.5 1.9 collective-permute-start
  18.4 1.3 constant_dynamic-update-slice_fusion.1
  19.7 1.3 constant_dynamic-update-slice_fusion
  21.6 1.2 reduce.7
  24.2 1.4 collective-permute-start.1
  26.3 4.3 %collective-permute-done.1 = f32[32,1,8,8]{2,3,0,1:T(8,128)S(1)} collective-permute-done((f32[32,1,8,8]{2,3,0,1:T(8,128)S(1)}, f32[32,1,8,8]{2,3,0,1:T(8,128)S(1)}, u32[]{:S(2)}, u32[]{:S(2)}) %collective-permute-start.1) | collective-permute-done | bytes 8224 | tf_op jit(solution)/shard_map/ppermute | solution.py:16
  32.4 33.3 %all-gather.2.cloned.1.call-done = bf16[256,4096]{1,0:T(8,128)(2,1)} async-done(((bf16[256,512]{1,0:T(8,128)(2,1)}), bf16[256,4096]{1,0:T(8,128)(2,1)}) %all-gather.2.cloned.1.call-update) | async-done | bytes 2097168 | tf_op jit(solution)/shard_map/all_gather | solution.py:115
  65.6 3.8 %convolution_bitcast_fusion.5 = f32[256,128]{0,1:T(8,128)S(1)} fusion(f32[128,4096]{1,0:T(8,128)S(1)} %constant_dynamic-update-slice_fusion, bf16[256,4096]{1,0:T(8,128)(2,1)} %all-gather.2.cloned.1.call-done), kind=kOutput, calls=%fused_computation.9 | convolution fusion | flops 1610612736 | bytes 4325376 | tf_op jit(solution)/shard_map/dot_general | solution.py:114
  70.3 5.1 %all-to-all-start.2 = ((f32[4,1,4096]{2,1,0:T(1,128)}), f32[4,1,4096]{2,1,0:T(1,128)}, u32[]{:S(2)}, u32[]{:S(2)}) async-start(f32[4,1,4096]{2,1,0:T(1,128)} %reshape.270), calls=%async_computation.3 | async-start | bytes 131072 | tf_op jit(solution)/shard_map/all_to_all | solution.py:52
  76.2 2.6 %all-to-all-done.2 = f32[4,1,4096]{2,1,0:T(1,128)} async-done(((f32[4,1,4096]{2,1,0:T(1,128)}), f32[4,1,4096]{2,1,0:T(1,128)}, u32[]{:S(2)}, u32[]{:S(2)}) %all-to-all-start.2) | async-done | bytes 65568 | tf_op jit(solution)/shard_map/all_to_all | solution.py:52
  78.8 1.7 reduce.6
  81.9 4.1 %all-to-all-start.1 = ((f32[4,1,4096]{2,1,0:T(1,128)}), f32[4,1,4096]{2,1,0:T(1,128)S(1)}, u32[]{:S(2)}, u32[]{:S(2)}) async-start(f32[4,1,4096]{2,1,0:T(1,128)} %reshape.268), calls=%async_computation.1 | async-start | bytes 131072 | tf_op jit(solution)/shard_map/all_to_all | solution.py:60
  86.1 1.7 fusion.43
  87.8 1.6 all-to-all-done.1
  90.5 5.0 %fusion.15 = f32[4096,256]{1,0:T(8,128)} fusion(f32[128,4096]{1,0:T(8,128)S(1)} %constant_dynamic-update-slice_fusion, f32[256,64]{0,1:T(8,128)S(1)} %copy.122, f32[256,64]{0,1:T(8,128)S(1)} %get-tuple-element.31), kind=kOutput, calls=%fused_computation.37 | convolution fusion | flops 1610645504 | bytes 6422528 | tf_op jit(solution)/shard_map/dot_general | solution.py:101
  96.0 1.2 collective-permute-start.3
  97.7 5.8 %collective-permute-done.3 = f32[32,1,8,9]{2,3,0,1:T(8,128)S(1)} collective-permute-done((f32[32,1,8,9]{2,3,0,1:T(8,128)S(1)}, f32[32,1,8,9]{2,3,0,1:T(8,128)S(1)}, u32[]{:S(2)}, u32[]{:S(2)}) %collective-permute-start.3) | collective-permute-done | bytes 9248 | tf_op jit(solution)/shard_map/ppermute | solution.py:16
  105.5 7.8 %all-to-all-start.3 = ((f32[4,1,12288]{2,1,0:T(1,128)}), f32[4,1,12288]{2,1,0:T(1,128)S(1)}, u32[]{:S(2)}, u32[]{:S(2)}) async-start(f32[4,1,12288]{2,1,0:T(1,128)} %reshape.272), calls=%async_computation.4 | async-start | bytes 393216 | tf_op jit(solution)/shard_map/all_to_all | solution.py:60
  113.8 2.3 %collective-permute-start.2 = (f32[1,1,256,257]{2,3,1,0:T(8,128)S(1)}, f32[1,1,256,257]{2,3,1,0:T(8,128)S(1)}, u32[]{:S(2)}, u32[]{:S(2)}) collective-permute-start(f32[1,1,256,257]{2,3,1,0:T(8,128)S(1)} %pad_maximum_fusion.2), channel_id=1, source_target_pairs={{0,1},{1,0},{2,3},{3,2},{4,5},{5,4},{6,7},{7,6},{8,9},{9,8},{10,11... | collective-permute-start | bytes 789512 | tf_op jit(solution)/shard_map/ppermute | solution.py:16
  116.1 1.8 all-to-all-done.3
  120.9 6.2 %collective-permute-done.2 = f32[1,1,256,257]{2,3,1,0:T(8,128)S(1)} collective-permute-done((f32[1,1,256,257]{2,3,1,0:T(8,128)S(1)}, f32[1,1,256,257]{2,3,1,0:T(8,128)S(1)}, u32[]{:S(2)}, u32[]{:S(2)}) %collective-permute-start.2) | collective-permute-done | bytes 263200 | tf_op jit(solution)/shard_map/ppermute | solution.py:16
  129.1 52.3 %reduce-scatter.2.cloned.1.call-done = f32[512,256]{1,0:T(8,128)} async-done(((f32[4096,256]{1,0:T(8,128)}), f32[512,256]{1,0:T(8,128)}) %reduce-scatter.2.cloned.1.call-update) | async-done | bytes 524304 | tf_op jit(solution)/shard_map/reduce_scatter | solution.py:100
  181.4 2.0 %copy.136 = f32[256,512]{1,0:T(8,128)} copy(f32[256,512]{0,1:T(8,128)} %bitcast.199) | data formatting | bytes 1048576
  (86 shorter events, 21.8 us)
Async XLA Ops:
  7.2 8.9 %copy-start.1 = (f32[256,64]{0,1:T(8,128)S(1)}, f32[256,64]{0,1:T(8,128)}, u32[]{:S(2)}) copy-start(f32[256,64]{0,1:T(8,128)} %param.7) | copy-start | bytes 196612
  7.2 8.9 %copy-start.3 = (f32[256,64]{0,1:T(8,128)S(1)}, f32[256,64]{0,1:T(8,128)}, u32[]{:S(2)}) copy-start(f32[256,64]{0,1:T(8,128)} %param.8) | copy-start | bytes 196612
  7.2 58.4 %all-gather.2.cloned.1.call-start = ((), (), s32[]{:S(2)}) async-start(), calls=%async_computation.6 | async-start | bytes 2359296 | tf_op jit(solution)/shard_map/all_gather | solution.py:115
  11.8 9.2 %all-to-all-start = ((f32[4,1,12288]{2,1,0:T(1,128)}), f32[4,1,12288]{2,1,0:T(1,128)S(1)}, u32[]{:S(2)}, u32[]{:S(2)}) async-start(f32[4,1,12288]{2,1,0:T(1,128)} %reshape.266), calls=%async_computation | async-start | bytes 393216 | tf_op jit(solution)/shard_map/all_to_all | solution.py:52
  16.5 14.3 %collective-permute-start = (f32[1,1,256,256]{2,3,1,0:T(8,128)S(1)}, f32[1,1,256,256]{2,3,1,0:T(8,128)S(1)}, u32[]{:S(2)}, u32[]{:S(2)}) collective-permute-start(f32[1,1,256,256]{2,3,1,0:T(8,128)S(1)} %convolution_bitcast_fusion.1), channel_id=1, source_target_pairs={{0,1},{1,0},{2,3},{3,2},{4,5},{5,4},{6,7},{7,6},{8,9},{9,8},{10,11... | collective-permute-start | bytes 786440 | tf_op jit(solution)/shard_map/ppermute | solution.py:16
  21.6 4.0 %copy-start.6 = (s32[4]{0:T(128)S(1)}, s32[4]{0:T(128)}, u32[]{:S(2)}) copy-start(s32[4]{0:T(128)} %param.10) | copy-start | bytes 52
  24.2 6.4 %collective-permute-start.1 = (f32[32,1,8,8]{2,3,0,1:T(8,128)S(1)}, f32[32,1,8,8]{2,3,0,1:T(8,128)S(1)}, u32[]{:S(2)}, u32[]{:S(2)}) collective-permute-start(f32[32,1,8,8]{2,3,0,1:T(8,128)S(1)} %convolution_bitcast_fusion.4), channel_id=1, source_target_pairs={{0,1},{1,0},{2,3},{3,2},{4,5},{5,4},{6,7},{7,6},{8,9},{9,8},{10,11... | collective-permute-start | bytes 24584 | tf_op jit(solution)/shard_map/ppermute | solution.py:16
  70.3 8.5 %all-to-all-start.2 = ((f32[4,1,4096]{2,1,0:T(1,128)}), f32[4,1,4096]{2,1,0:T(1,128)}, u32[]{:S(2)}, u32[]{:S(2)}) async-start(f32[4,1,4096]{2,1,0:T(1,128)} %reshape.270), calls=%async_computation.3 | async-start | bytes 131072 | tf_op jit(solution)/shard_map/all_to_all | solution.py:52
  81.9 7.4 %all-to-all-start.1 = ((f32[4,1,4096]{2,1,0:T(1,128)}), f32[4,1,4096]{2,1,0:T(1,128)S(1)}, u32[]{:S(2)}, u32[]{:S(2)}) async-start(f32[4,1,4096]{2,1,0:T(1,128)} %reshape.268), calls=%async_computation.1 | async-start | bytes 131072 | tf_op jit(solution)/shard_map/all_to_all | solution.py:60
  86.1 95.4 %reduce-scatter.2.cloned.1.call-start = ((), (), s32[]{:S(2)}) async-start(), calls=%async_computation.5 | async-start | bytes 4718592 | tf_op jit(solution)/shard_map/reduce_scatter | solution.py:100
  96.0 7.5 %collective-permute-start.3 = (f32[32,1,8,9]{2,3,0,1:T(8,128)S(1)}, f32[32,1,8,9]{2,3,0,1:T(8,128)S(1)}, u32[]{:S(2)}, u32[]{:S(2)}) collective-permute-start(f32[32,1,8,9]{2,3,0,1:T(8,128)S(1)} %pad_maximum_fusion.3), channel_id=1, source_target_pairs={{0,1},{1,0},{2,3},{3,2},{4,5},{5,4},{6,7},{7,6},{8,9},{9,8},{10,11... | collective-permute-start | bytes 27656 | tf_op jit(solution)/shard_map/ppermute | solution.py:16
  97.7 15.7 %copy-start = (f32[256,64]{0,1:T(8,128)S(1)}, f32[256,64]{0,1:T(8,128)}, u32[]{:S(2)}) copy-start(f32[256,64]{0,1:T(8,128)} %param.9) | copy-start | bytes 196612
  97.7 16.1 %copy-start.5 = (f32[256]{0:T(256)S(1)}, f32[256]{0:T(256)}, u32[]{:S(2)}) copy-start(f32[256]{0:T(256)} %get-tuple-element.30) | copy-start | bytes 3076
  105.5 12.4 %all-to-all-start.3 = ((f32[4,1,12288]{2,1,0:T(1,128)}), f32[4,1,12288]{2,1,0:T(1,128)S(1)}, u32[]{:S(2)}, u32[]{:S(2)}) async-start(f32[4,1,12288]{2,1,0:T(1,128)} %reshape.272), calls=%async_computation.4 | async-start | bytes 393216 | tf_op jit(solution)/shard_map/all_to_all | solution.py:60
  113.8 13.3 %collective-permute-start.2 = (f32[1,1,256,257]{2,3,1,0:T(8,128)S(1)}, f32[1,1,256,257]{2,3,1,0:T(8,128)S(1)}, u32[]{:S(2)}, u32[]{:S(2)}) collective-permute-start(f32[1,1,256,257]{2,3,1,0:T(8,128)S(1)} %pad_maximum_fusion.2), channel_id=1, source_target_pairs={{0,1},{1,0},{2,3},{3,2},{4,5},{5,4},{6,7},{7,6},{8,9},{9,8},{10,11... | collective-permute-start | bytes 789512 | tf_op jit(solution)/shard_map/ppermute | solution.py:16
  119.3 7.8 %copy-start.2 = (f32[256,64]{0,1:T(8,128)S(1)}, f32[256,64]{0,1:T(8,128)}, u32[]{:S(2)}) copy-start(f32[256,64]{0,1:T(8,128)} %param.7) | copy-start | bytes 196612
  119.4 8.8 %copy-start.4 = (f32[256,64]{0,1:T(8,128)S(1)}, f32[256,64]{0,1:T(8,128)}, u32[]{:S(2)}) copy-start(f32[256,64]{0,1:T(8,128)} %param.8) | copy-start | bytes 196612
Sparse Core Ops, SparseCore 0:
  10.1 55.5 all-gather.1
  95.6 85.7 reduce-scatter.1
where the time goes:
time: 192 us; the launch traced here: 190 us
  waiting for transfers between devices  109 us (57%)
  starting transfers between devices  28.1 us (15%)
  matrix products  17.1 us (9%)
  between operations  14.5 us (8%)
  local copies, waits for them, and re-layouts  14.4 us (8%)
  other arithmetic  7.59 us (4%)
    reduce_scatter x1, waiting for transfers between devices, local(): lax.psum_scatter(lax.dot_general(w_cols, attn_both, (((0,), (1,)), ((), (...  52.3 us
    all_gather x1, waiting for transfers between devices, local(): lax.all_gather(grad_out, 'head', axis=1, tiled=True).astype(jnp.float32)  33.3 us
    ppermute x4, waiting for transfers between devices, swapped(): lax.ppermute(x, axis, [(i, i ^ 1 << distance) for i in range(lax.axis_siz...  16.4 us
    all_to_all x2, starting transfers between devices, to_contiguous(): lax.all_to_all(layout, 'seq', split_axis=0, concat_axis=2, tiled=True)  12 us
    unnamed x30, local copies, waits for them, and re-layouts  10.5 us
    all_to_all x2, starting transfers between devices, to_strided(): lax.all_to_all(layout, 'seq', split_axis=1, concat_axis=0, tiled=True)  9.39 us
    ppermute x4, starting transfers between devices, swapped(): lax.ppermute(x, axis, [(i, i ^ 1 << distance) for i in range(lax.axis_siz...  6.72 us
    dot_general x1, matrix products, local(): lax.dot_general(w_cols, attn_both, (((0,), (1,)), ((), ())), precision=HI...  5 us
  transfers between devices with their start and end apart: 10, of which 8 were waited for; matrix products, arithmetic and copies ran while one was open for 12% of the time, Pallas kernels for 0%

commit v1 on v0

v1 whole, which is shorter than its diff:
```python
import functools

import jax
import jax.numpy as jnp
from jax import lax
from jax.experimental import pallas as pl
from jax.experimental.pallas import tpu as pltpu
from jax.sharding import PartitionSpec as P

HDIM = 128
STRIDE = 128
HALF = HDIM // 2
RUNS = 2
HIGHEST = lax.Precision.HIGHEST
NN = (((1,), (0,)), ((), ()))
NT = (((1,), (1,)), ((), ()))
TN = (((0,), (0,)), ((), ()))


def exact_dot(a, b, dims):
    return lax.dot_general(a, b, dims, precision=HIGHEST, preferred_element_type=jnp.float32)


def bf16_dot(a, b, dims):
    return lax.dot_general(a, b, dims, preferred_element_type=jnp.float32)


def halves(x):
    high = x.astype(jnp.bfloat16)
    return high, (x - high.astype(jnp.float32)).astype(jnp.bfloat16)


def split_dot(a, b, dims):
    (a_high, a_low), (b_high, b_low) = halves(a), halves(b)
    return bf16_dot(a_high, b_high, dims) + (
        bf16_dot(a_high, b_low, dims) + bf16_dot(a_low, b_high, dims)
    )


def kernel(
    seqs, heads, share,
    span_ref, pack_ref, gout_ref, wo_local_ref, wo_strided_ref,
    mixed_ref, grads_ref,
    w_buf, pack_buf, gout_buf, q_buf, k_buf, v_buf, p_buf, attn_own, attn_buf,
    gpart, g_buf, m_buf, m_recv, e_out, e_buf,
    w_send, w_recv, share_send, pack_send, pack_recv, gout_send, gout_recv,
    attn_send, attn_recv, g_send, g_recv, m_send, m_recv_sem, e_send, e_recv,
):
    pairs = heads // 2
    res = STRIDE // seqs
    piece = RUNS * res
    rows = seqs * piece
    w_rows = HALF // share
    width = gout_ref.shape[1]
    me_s = lax.axis_index("seq")
    me_h = lax.axis_index("head")
    pair = lax.div(me_h, 2)
    side = lax.rem(me_h, 2)
    partner = me_h + 1 - 2 * side
    quarter = lax.rem(me_s, share)

    def to_seq(t):
        return (1 - side) * me_s + side * t

    def to_slot(t):
        return (1 - side) * t + side * me_s

    def flip(value, distance):
        return value + distance - 2 * distance * lax.rem(lax.div(value, distance), 2)

    def is_me(s, h):
        return jnp.logical_and(s == me_s, h == me_h)

    def remote(src, dst, send_sem, recv_sem, s, h):
        return pltpu.make_async_remote_copy(
            src_ref=src, dst_ref=dst, send_sem=send_sem, recv_sem=recv_sem,
            device_id=(s, h), device_id_type=pl.DeviceIdType.MESH,
        )

    def send(src, dst, send_sem, recv_sem, s, h):
        same = is_me(s, h)

        @pl.when(same)
        def _():
            pltpu.make_async_copy(src, dst, recv_sem).start()

        @pl.when(jnp.logical_not(same))
        def _():
            remote(src, dst, send_sem, recv_sem, s, h).start()

    def sent(src, dst, send_sem, recv_sem, s, h):
        @pl.when(jnp.logical_not(is_me(s, h)))
        def _():
            remote(src, dst, send_sem, recv_sem, s, h).wait_send()

    def arrived(dst, recv_sem):
        pltpu.make_async_copy(dst, dst, recv_sem).wait()

    def loop(count, body):
        def step(i, carry):
            body(i)
            return carry
        lax.fori_loop(0, count, step, 0)

    barrier = pltpu.get_barrier_semaphore()

    def greet(i):
        s, h = lax.div(i, heads), lax.rem(i, heads)
        near = jnp.logical_or(s == me_s, lax.div(h, 2) == pair)
        odd = jnp.logical_and(lax.rem(h, 2) == 1, side == 1)
        wanted = jnp.logical_or(near, odd)

        @pl.when(jnp.logical_and(wanted, jnp.logical_not(is_me(s, h))))
        def _():
            pl.semaphore_signal(
                barrier, inc=1, device_id=(s, h), device_id_type=pl.DeviceIdType.MESH
            )

    loop(seqs * heads, greet)
    pl.semaphore_wait(
        barrier, heads - 1 + 2 * (seqs - 1) + side * (seqs - 1) * (pairs - 1)
    )

    def pack_copies(act, t):
        for other in range(2):
            s = (1 - other) * me_s + other * t
            slot = (1 - other) * t + other * me_s
            act(
                pack_ref.at[t], pack_buf.at[side, slot], pack_send.at[other, t],
                pack_recv.at[side, slot], s, 2 * pair + other,
            )

    loop(seqs, functools.partial(pack_copies, send))

    def w_copies(act, step):
        z = lax.rem(step + pair, pairs)
        own_rows = pl.ds(pl.multiple_of(quarter * w_rows, 8), w_rows)
        cols = pl.ds(pl.multiple_of(z * 2 * width, 128), 2 * width)
        for other, source in ((0, wo_local_ref), (1, wo_strided_ref)):
            act(
                source.at[own_rows, cols], w_buf.at[me_h, quarter], w_send.at[z, other],
                w_recv.at[me_h, quarter], me_s, 2 * z + other,
            )

    loop(pairs, functools.partial(w_copies, send))

    gout_copy = remote(
        gout_ref, gout_buf.at[side], gout_send.at[0], gout_recv.at[0], me_s, partner
    )
    gout_copy.start()
    gout_buf[side] = gout_ref[...]

    def share_copy(act, j, stage, offset_at, offset, distance):
        q = quarter
        for bit in (1, 2, 4, 8, 16, 32):
            if offset & bit:
                q = flip(q, bit)
        act(
            w_buf.at[j, q], w_buf.at[j, q], share_send.at[j, stage + offset_at],
            w_recv.at[j, q], flip(me_s, distance), me_h,
        )

    def w_arrived(j, offset):
        q = quarter
        for bit in (1, 2, 4, 8, 16, 32):
            if offset & bit:
                q = flip(q, bit)
        arrived(w_buf.at[j, q], w_recv.at[j, q])

    stages, held, fresh, distance = [], [0], [0], share // 2
    while distance:
        stages.append((distance, tuple(held), tuple(fresh)))
        fresh = [offset ^ distance for offset in held]
        held = held + fresh
        distance //= 2

    def run_stage(at):
        distance, held_here, fresh_here = stages[at]
        first = sum(len(s[1]) for s in stages[:at])

        def body(j):
            for n, offset in enumerate(held_here):
                if offset in fresh_here:
                    w_arrived(j, offset)
                share_copy(send, j, first, n, offset, distance)

        loop(heads, body)

    run_stage(0)

    for c in range(2):
        for t in range(seqs):
            arrived(pack_buf.at[c, t], pack_recv.at[c, t])

    lane = lax.broadcasted_iota(jnp.int32, (rows, HDIM), 1) < HALF
    lane_half = lax.broadcasted_iota(jnp.int32, (rows // 2, HDIM), 1) < HALF

    def turn(x):
        return pltpu.roll(x, HALF, 1)

    qk_first = pack_buf[0, :, :RUNS].reshape(rows, HDIM)
    qk_second = pack_buf[1, :, :RUNS].reshape(rows, HDIM)
    q_buf[...] = jnp.where(lane, qk_first, turn(qk_second))
    k_buf[...] = jnp.where(lane, turn(qk_first), qk_second)
    v_first = pack_buf[0, :, RUNS].reshape(rows // 2, HDIM)
    v_second = pack_buf[1, :, RUNS].reshape(rows // 2, HDIM)
    v_buf[:, 0] = jnp.where(lane_half, v_first, turn(v_second)).reshape(seqs, res, HDIM)
    v_buf[:, 1] = jnp.where(lane_half, turn(v_first), v_second).reshape(seqs, res, HDIM)

    res_bits = res.bit_length() - 1

    def place(dim):
        index = lax.broadcasted_iota(jnp.int32, (rows, rows), dim)
        run = (index >> res_bits) & 1
        part = index >> (res_bits + 1)
        residue = index & (res - 1)
        return run, part, residue

    run_i, part_i, residue_i = place(0)
    run_j, part_j, residue_j = place(1)
    at_i = run_i * STRIDE + part_i * res + residue_i
    at_j = run_j * STRIDE + part_j * res + residue_j
    local_ok = jnp.where((at_j <= at_i) & (run_i - run_j < span_ref[pair]), 1, 0)
    order_ok = RUNS * part_j + run_j <= RUNS * part_i + run_i
    strided_ok = jnp.where((residue_i == residue_j) & order_ok, 1, 0)
    allowed = local_ok * (1 - side) + strided_ok * side > 0

    scale = HDIM ** (-0.5)
    scores = exact_dot(q_buf[...], k_buf[...], NT) * scale
    row_max = jnp.max(jnp.where(allowed, scores, -jnp.inf), axis=-1, keepdims=True)
    weights = jnp.where(allowed, jnp.exp(scores - row_max), 0.0)
    probs = weights / jnp.sum(weights, axis=-1, keepdims=True)
    p_buf[...] = probs
    attended = exact_dot(probs, v_buf[...].reshape(rows, HDIM), NN)
    attn_own[...] = attended.reshape(seqs, piece, HDIM)

    def attn_copies(act, step):
        z = lax.rem(step + pair, pairs)

        def one(t):
            act(
                attn_own.at[t], attn_buf.at[pair, to_slot(t)], attn_send.at[z, t],
                attn_recv.at[pair, to_slot(t)], to_seq(t), 2 * z + side,
            )

        loop(seqs, one)

    loop(pairs, functools.partial(attn_copies, send))

    for at in range(1, len(stages)):
        run_stage(at)

    def last_of_w(j):
        for offset in fresh:
            w_arrived(j, offset)

    loop(heads, last_of_w)

    gout_copy.wait_recv()

    def head_rows(g):
        return w_buf[pl.ds(2 * g, 2)].reshape(HDIM, 2 * width)

    def g_copies(act, g):
        def one(t):
            act(
                gpart.at[g, t], g_buf.at[pair, to_slot(t)], g_send.at[g, t],
                g_recv.at[pair, to_slot(t)], to_seq(t), 2 * g + side,
            )

        loop(seqs, one)

    def partial_grad(step):
        g = lax.rem(step + pair, pairs)
        w_high, w_low = halves(head_rows(g))
        total = jnp.zeros((rows, HDIM), jnp.float32)
        for c in range(2):
            cols = slice(c * width, (c + 1) * width)
            out = gout_buf[c]
            total = total + (
                bf16_dot(out, w_high[:, cols], NT) + bf16_dot(out, w_low[:, cols], NT)
            )
        gpart[g] = total.reshape(seqs, piece, HDIM)
        g_copies(send, g)

    loop(pairs, partial_grad)

    m_buf[...] = jnp.zeros_like(m_buf)

    def partial_mixed(g):
        loop(seqs, lambda t: arrived(attn_buf.at[g, t], attn_recv.at[g, t]))
        a_high, a_low = halves(attn_buf[g].reshape(rows, HDIM))
        w_high, w_low = halves(head_rows(g))
        for c in range(2):
            cols = slice(c * width, (c + 1) * width)
            m_buf[c] += bf16_dot(a_high, w_high[:, cols], NN) + (
                bf16_dot(a_high, w_low[:, cols], NN) + bf16_dot(a_low, w_high[:, cols], NN)
            )

    loop(pairs, partial_mixed)
    m_copy = remote(
        m_buf.at[1 - side], m_recv, m_send.at[0], m_recv_sem.at[0], me_s, partner
    )
    m_copy.start()

    def g_arrived(z):
        loop(seqs, lambda t: arrived(g_buf.at[z, t], g_recv.at[z, t]))

    loop(pairs, g_arrived)
    incoming = jnp.sum(g_buf[...], axis=0).reshape(rows, HDIM)
    delta = jnp.sum(incoming * attn_own[...].reshape(rows, HDIM), axis=-1, keepdims=True)
    dprobs = exact_dot(incoming, v_buf[...].reshape(rows, HDIM), NT)
    probs = p_buf[...]
    dscores = probs * (dprobs - delta)
    dq = split_dot(dscores, k_buf[...], NN) * scale
    dk = split_dot(dscores, q_buf[...], TN) * scale
    dv = split_dot(probs, incoming, TN).reshape(seqs, RUNS, res, HDIM)
    e_out[0, :, :RUNS] = jnp.where(lane, dq, turn(dk)).reshape(seqs, RUNS, res, HDIM)
    e_out[1, :, :RUNS] = jnp.where(lane, turn(dq), dk).reshape(seqs, RUNS, res, HDIM)
    dv_first = dv[:, 0].reshape(rows // 2, HDIM)
    dv_second = dv[:, 1].reshape(rows // 2, HDIM)
    e_out[0, :, RUNS] = jnp.where(lane_half, dv_first, turn(dv_second)).reshape(seqs, res, HDIM)
    e_out[1, :, RUNS] = jnp.where(lane_half, turn(dv_first), dv_second).reshape(seqs, res, HDIM)

    def e_copies(act, t):
        for c in range(2):
            act(
                e_out.at[c, t], e_buf.at[side, to_slot(t)], e_send.at[c, t],
                e_recv.at[side, to_slot(t)], to_seq(t), 2 * pair + c,
            )

    loop(seqs, functools.partial(e_copies, send))

    m_copy.wait_recv()
    mixed_ref[...] = m_buf[side] + m_recv[...]

    for c in range(2):
        for t in range(seqs):
            arrived(e_buf.at[c, t], e_recv.at[c, t])
    grads_ref[...] = e_buf[0] + e_buf[1]

    loop(seqs, functools.partial(pack_copies, sent))
    loop(pairs, functools.partial(w_copies, sent))
    gout_copy.wait_send()
    first = 0
    for distance, held_here, _ in stages:
        def left(j, distance=distance, held_here=held_here, first=first):
            for n, offset in enumerate(held_here):
                share_copy(sent, j, first, n, offset, distance)

        loop(heads, left)
        first += len(held_here)
    loop(pairs, functools.partial(attn_copies, sent))
    loop(pairs, functools.partial(g_copies, sent))
    m_copy.wait_send()
    loop(seqs, functools.partial(e_copies, sent))


def local(queries, keys, values, local_span, wo_local, wo_strided, grad_out):
    seqs, heads = lax.axis_size("seq"), lax.axis_size("head")
    rows, width = grad_out.shape
    res = STRIDE // seqs
    pairs = heads // 2
    share = min(seqs, HALF // 8)
    piece = RUNS * res
    query_key = jnp.concatenate([queries, keys], axis=1).reshape(RUNS, seqs, res, HDIM)
    value_pair = jnp.concatenate([values[: rows // 2], values[rows // 2 :]], axis=1)
    packed = jnp.concatenate([query_key, value_pair.reshape(1, seqs, res, HDIM)], axis=0)
    packed = packed.transpose(1, 0, 2, 3)
    cotangent = grad_out.reshape(RUNS, seqs, res, width).transpose(1, 0, 2, 3)
    cotangent = cotangent.reshape(rows, width)
    vmem = pl.BlockSpec(memory_space=pltpu.VMEM)
    hbm = pl.BlockSpec(memory_space=pl.ANY)
    dma = pltpu.SemaphoreType.DMA
    f32 = jnp.float32
    mixed, grads = pl.pallas_call(
        functools.partial(kernel, seqs, heads, share),
        out_shape=(
            jax.ShapeDtypeStruct((rows, width), f32),
            jax.ShapeDtypeStruct((seqs, RUNS + 1, res, HDIM), f32),
        ),
        in_specs=[pl.BlockSpec(memory_space=pltpu.SMEM), vmem, vmem, hbm, hbm],
        out_specs=(vmem, vmem),
        scratch_shapes=[
            pltpu.VMEM((heads, share, HALF // share, 2 * width), f32),
            pltpu.VMEM((2, seqs, RUNS + 1, res, HDIM), f32),
            pltpu.VMEM((2, rows, width), jnp.bfloat16),
            pltpu.VMEM((rows, HDIM), f32),
            pltpu.VMEM((rows, HDIM), f32),
            pltpu.VMEM((seqs, RUNS, res, HDIM), f32),
            pltpu.VMEM((rows, rows), f32),
            pltpu.VMEM((seqs, piece, HDIM), f32),
            pltpu.VMEM((pairs, seqs, piece, HDIM), f32),
            pltpu.VMEM((pairs, seqs, piece, HDIM), f32),
            pltpu.VMEM((pairs, seqs, piece, HDIM), f32),
            pltpu.VMEM((2, rows, width), f32),
            pltpu.VMEM((rows, width), f32),
            pltpu.VMEM((2, seqs, RUNS + 1, res, HDIM), f32),
            pltpu.VMEM((2, seqs, RUNS + 1, res, HDIM), f32),
            dma((pairs, 2)),
            dma((heads, share)),
            dma((heads, share)),
            dma((2, seqs)),
            dma((2, seqs)),
            dma((1,)),
            dma((1,)),
            dma((pairs, seqs)),
            dma((pairs, seqs)),
            dma((pairs, seqs)),
            dma((pairs, seqs)),
            dma((1,)),
            dma((1,)),
            dma((2, seqs)),
            dma((2, seqs)),
        ],
        compiler_params=pltpu.CompilerParams(
            collective_id=0, has_side_effects=True, vmem_limit_bytes=48 * 1024 * 1024
        ),
        cost_estimate=pl.CostEstimate(
            flops=2 * rows * 2 * width * HDIM * pairs * 5,
            bytes_accessed=16 * rows * width,
            transcendentals=rows * rows,
        ),
    )(local_span, packed, cotangent, wo_local, wo_strided)
    mixed = mixed.reshape(seqs, RUNS, res, width).transpose(1, 0, 2, 3).reshape(rows, width)
    grads = grads.transpose(1, 0, 2, 3).reshape(RUNS + 1, rows // RUNS, HDIM)
    grad_queries = grads[:RUNS, :, :HALF].reshape(rows, HALF)
    grad_keys = grads[:RUNS, :, HALF:].reshape(rows, HALF)
    grad_values = jnp.concatenate([grads[RUNS, :, :HALF], grads[RUNS, :, HALF:]], axis=0)
    return (mixed, grad_queries, grad_keys, grad_values)


def solution(mesh):
    return jax.shard_map(
        local,
        mesh=mesh,
        in_specs=(
            P("seq", "head"),
            P("seq", "head"),
            P("seq", "head"),
            P(),
            P("head", None),
            P("head", None),
            P("seq", "head"),
        ),
        out_specs=(P("seq", "head"), P("seq", "head"), P("seq", "head"), P("seq", "head")),
        check_vma=False,
    )
```

time: 192 us -> 72.6 us (0.38)
  waiting for transfers between devices: 109 us -> 0 us
  Pallas kernels: 0 us -> 63.8 us
  starting transfers between devices: 28.1 us -> 0 us
  matrix products: 17.1 us -> 0 us
  between operations: 14.5 us -> 0.74 us
  other arithmetic: 7.59 us -> 0.14 us
  local copies, waits for them, and re-layouts: 14.4 us -> 7.66 us
    pallas_call x0 -> x1, Pallas kernels: none -> 63.8 us  [local(): pl.pallas_call(functools.partial(kernel, seqs, heads, share), out_shape=(...]
    reduce_scatter x1 -> x0, waiting for transfers between devices: 52.3 us -> none  [local(): lax.psum_scatter(lax.dot_general(w_cols, attn_both, (((0,), (1,)), ((), (...]
    all_gather x1 -> x0, waiting for transfers between devices: 33.3 us -> none  [local(): lax.all_gather(grad_out, 'head', axis=1, tiled=True).astype(jnp.float32)]
    all_to_all x4 -> x0, starting transfers between devices: 21.3 us -> none  [the longest x2 12 us: to_contiguous(): lax.all_to_all(layout, 'seq', split_axis=0, concat_axis=2, tiled=True)]
    dot_general x14 -> x0, matrix products: 17.1 us -> none  [the longest x1 5 us: local(): lax.dot_general(w_cols, attn_both, (((0,), (1,)), ((), ())), precision=HI...]
    ppermute x4 -> x0, waiting for transfers between devices: 16.4 us -> none  [swapped(): lax.ppermute(x, axis, [(i, i ^ 1 << distance) for i in range(lax.axis_siz...]
    unnamed x30 -> x9, local copies, waits for them, and re-layouts: 10.5 us -> 3.22 us
    ppermute x4 -> x0, starting transfers between devices: 6.72 us -> none  [swapped(): lax.ppermute(x, axis, [(i, i ^ 1 << distance) for i in range(lax.axis_siz...]
  transfers between devices with their start and end apart: 10 -> 0, of which waited for: 8 -> 0; matrix products, arithmetic and copies ran while one was open for 12% -> 0% of each run, Pallas kernels for 0% -> 0%
where the time goes in v1:
time: 72.6 us; the launch traced here: 72.3 us
  Pallas kernels  63.8 us (88%)
  local copies, waits for them, and re-layouts  7.66 us (11%)
  between operations  0.74 us (1%)
    pallas_call x1, Pallas kernels, local(): pl.pallas_call(functools.partial(kernel, seqs, heads, share), out_shape=(...  63.8 us
    unnamed x9, local copies, waits for them, and re-layouts  3.22 us

profile of v1, /device:TPU:1, one launch (start us, length us, event | category | flops | bytes accessed | tf_op | source)
XLA Modules:
  0.0 72.3 jit_solution(7755734199251856663)
XLA Ops:
  0.6 0.0 copy-start
  0.6 0.0 copy-start.1
  0.7 0.9 %fusion.1 = (f32[128,64]{0,1:T(8,128)S(1)}, f32[128,64]{0,1:T(8,128)S(1)}) fusion(f32[256,64]{0,1:T(8,128)} %param.9), kind=kLoop, calls=%fused_computation.7 | loop fusion | bytes 131072 | tf_op jit(solution)/shard_map/slice | solution.py:367
  1.6 0.1 copy.16
  1.7 0.9 %copy.14 = f32[256,64]{1,0:T(8,128)S(1)} copy(f32[256,64]{0,1:T(8,128)} %param.7) | data formatting | bytes 131072 | tf_op args[0]
  2.6 0.9 %copy.15 = f32[256,64]{1,0:T(8,128)S(1)} copy(f32[256,64]{0,1:T(8,128)} %param.8) | data formatting | bytes 131072 | tf_op args[1]
  3.6 0.1 pad_maximum_fusion
  3.7 1.0 %copy.18 = bf16[2,4,32,512]{3,2,0,1:T(8,128)(2,1)S(1)} copy(bf16[2,4,32,512]{3,2,1,0:T(8,128)(2,1)} %bitcast.29) | data formatting | bytes 524288 | tf_op jit(solution)/shard_map/reshape | solution.py:370
  4.7 0.0 copy-start.2
  4.7 0.0 copy-done
  4.7 0.0 copy-done.1
  4.7 0.6 copy-done.2
  5.3 63.8 %shard_map.102 = (f32[256,512]{1,0:T(8,128)S(1)}, f32[4,3,32,128]{3,2,1,0:T(8,128)S(1)}) custom-call(s32[4]{0:T(128)S(1)} %copy-done.2, f32[4,3,32,128]{3,2,1,0:T(8,128)S(1)} %maximum_bitcast_fusion.pack_ref, bf16[256,512]{1,0:T(8,128)(2,1)S(1)} %bitcast.21, f32[64,4096]{1,0:T(8,128)S(1)} %copy-done, f32[64,4096]{1,0:T(8,128)S(1)} %copy-done.1), custom_call_target="tpu_custom_call" | custom-call | flops 1342177280 | bytes 2097152 | tf_op jit(solution)/shard_map/pallas_call | solution.py:376
  69.1 0.8 %copy.19 = f32[2,4,32,512]{3,2,1,0:T(8,128)} copy(f32[2,4,32,512]{3,2,0,1:T(8,128)S(1)} %bitcast.20) | data formatting | bytes 1048576 | tf_op jit(solution)/shard_map/transpose | solution.py:425
  70.0 0.1 slice_bitcast_fusion.1
  70.1 0.7 copy.23
  70.8 0.1 fusion
  70.9 0.7 copy.25
  71.6 0.7 copy.24
  (4 shorter events, 0.1 us)
Async XLA Ops:
  0.6 4.1 %copy-start = (f32[64,4096]{1,0:T(8,128)S(1)}, f32[64,4096]{1,0:T(8,128)}, u32[]{:S(2)}) copy-start(f32[64,4096]{1,0:T(8,128)} %wo_local_ref.1) | copy-start | bytes 3145732
  0.6 4.1 %copy-start.1 = (f32[64,4096]{1,0:T(8,128)S(1)}, f32[64,4096]{1,0:T(8,128)}, u32[]{:S(2)}) copy-start(f32[64,4096]{1,0:T(8,128)} %wo_strided_ref.1) | copy-start | bytes 3145732
  4.7 0.7 copy-start.2

commit v2 on v1

--- a/solution.py
+++ b/solution.py
@@ -39,17 +39,16 @@
 
 def kernel(
     seqs, heads, share,
-    span_ref, pack_ref, gout_ref, wo_local_ref, wo_strided_ref,
-    mixed_ref, grads_ref,
-    w_buf, pack_buf, gout_buf, q_buf, k_buf, v_buf, p_buf, attn_own, attn_buf,
+    span_ref, query_ref, key_ref, value_ref, gout_ref, wo_local_ref, wo_strided_ref,
+    mixed_ref, grad_query_ref, grad_key_ref, grad_value_ref,
+    w_buf, pack_ref, pack_buf, gout_buf, q_buf, k_buf, v_buf, p_buf, attn_own, attn_buf,
     gpart, g_buf, m_buf, m_recv, e_out, e_buf,
     w_send, w_recv, share_send, pack_send, pack_recv, gout_send, gout_recv,
     attn_send, attn_recv, g_send, g_recv, m_send, m_recv_sem, e_send, e_recv,
 ):
     pairs = heads // 2
     res = STRIDE // seqs
-    piece = RUNS * res
-    rows = seqs * piece
+    rows = seqs * RUNS * res
     w_rows = HALF // share
     width = gout_ref.shape[1]
     me_s = lax.axis_index("seq")
@@ -68,6 +67,13 @@
     def flip(value, distance):
         return value + distance - 2 * distance * lax.rem(lax.div(value, distance), 2)
 
+    def exclusive(one, two):
+        total, bit = one + two, 1
+        while bit < pairs:
+            total = total - 2 * bit * lax.rem(lax.div(one, bit), 2) * lax.rem(lax.div(two, bit), 2)
+            bit *= 2
+        return total
+
     def is_me(s, h):
         return jnp.logical_and(s == me_s, h == me_h)
 
@@ -117,6 +123,13 @@
             )
 
     loop(seqs * heads, greet)
+
+    query_key = jnp.concatenate([query_ref[...], key_ref[...]], axis=0).T
+    for a in range(RUNS):
+        pack_ref[:, a] = query_key[a * STRIDE : (a + 1) * STRIDE].reshape(seqs, res, HDIM)
+    value_pair = jnp.concatenate([value_ref[:, :STRIDE], value_ref[:, STRIDE:]], axis=0).T
+    pack_ref[:, RUNS] = value_pair.reshape(seqs, res, HDIM)
+
     pl.semaphore_wait(
         barrier, heads - 1 + 2 * (seqs - 1) + side * (seqs - 1) * (pairs - 1)
     )
@@ -133,7 +146,7 @@
     loop(seqs, functools.partial(pack_copies, send))
 
     def w_copies(act, step):
-        z = lax.rem(step + pair, pairs)
+        z = exclusive(step, pair)
         own_rows = pl.ds(pl.multiple_of(quarter * w_rows, 8), w_rows)
         cols = pl.ds(pl.multiple_of(z * 2 * width, 128), 2 * width)
         for other, source in ((0, wo_local_ref), (1, wo_strided_ref)):
@@ -174,19 +187,59 @@
         held = held + fresh
         distance //= 2
 
-    def run_stage(at):
+    def run_stage(at, z):
         distance, held_here, fresh_here = stages[at]
         first = sum(len(s[1]) for s in stages[:at])
-
-        def body(j):
+        for c in range(2):
+            j = 2 * z + c
             for n, offset in enumerate(held_here):
                 if offset in fresh_here:
                     w_arrived(j, offset)
                 share_copy(send, j, first, n, offset, distance)
 
-        loop(heads, body)
-
-    run_stage(0)
+    def head_rows(g):
+        return w_buf[pl.ds(2 * g, 2)].reshape(HDIM, 2 * width)
+
+    def g_copies(act, g):
+        def one(t):
+            act(
+                gpart.at[g, t], g_buf.at[pair, to_slot(t)], g_send.at[g, t],
+                g_recv.at[pair, to_slot(t)], to_seq(t), 2 * g + side,
+            )
+
+        loop(seqs, one)
+
+    def partial_grad(g):
+        for offset in fresh:
+            for c in range(2):
+                w_arrived(2 * g + c, offset)
+        w_high, w_low = halves(head_rows(g))
+        total = jnp.zeros((rows, HDIM), jnp.float32)
+        for c in range(2):
+            cols = slice(c * width, (c + 1) * width)
+            out = gout_buf[c]
+            total = total + (
+                bf16_dot(out, w_high[:, cols], NT) + bf16_dot(out, w_low[:, cols], NT)
+            )
+        for a in range(RUNS):
+            gpart[g, :, a] = total[a * STRIDE : (a + 1) * STRIDE].reshape(seqs, res, HDIM)
+        g_copies(send, g)
+
+    def w_step(step):
+        for at in range(len(stages) + 1):
+            turn_of = step - at
+
+            @pl.when(jnp.logical_and(turn_of >= 0, turn_of < pairs))
+            def _(at=at, turn_of=turn_of):
+                z = exclusive(turn_of, pair)
+                if at < len(stages):
+                    run_stage(at, z)
+                else:
+                    partial_grad(z)
+
+    ahead = min(2, len(stages))
+
+    loop(ahead, w_step)
 
     for c in range(2):
         for t in range(seqs):
@@ -232,10 +285,10 @@
     probs = weights / jnp.sum(weights, axis=-1, keepdims=True)
     p_buf[...] = probs
     attended = exact_dot(probs, v_buf[...].reshape(rows, HDIM), NN)
-    attn_own[...] = attended.reshape(seqs, piece, HDIM)
+    attn_own[...] = attended.reshape(seqs, RUNS, res, HDIM)
 
     def attn_copies(act, step):
-        z = lax.rem(step + pair, pairs)
+        z = exclusive(step, pair)
 
         def one(t):
             act(
@@ -247,49 +300,22 @@
 
     loop(pairs, functools.partial(attn_copies, send))
 
-    for at in range(1, len(stages)):
-        run_stage(at)
-
-    def last_of_w(j):
-        for offset in fresh:
-            w_arrived(j, offset)
-
-    loop(heads, last_of_w)
-
     gout_copy.wait_recv()
 
-    def head_rows(g):
-        return w_buf[pl.ds(2 * g, 2)].reshape(HDIM, 2 * width)
-
-    def g_copies(act, g):
-        def one(t):
-            act(
-                gpart.at[g, t], g_buf.at[pair, to_slot(t)], g_send.at[g, t],
-                g_recv.at[pair, to_slot(t)], to_seq(t), 2 * g + side,
-            )
-
-        loop(seqs, one)
-
-    def partial_grad(step):
-        g = lax.rem(step + pair, pairs)
-        w_high, w_low = halves(head_rows(g))
-        total = jnp.zeros((rows, HDIM), jnp.float32)
-        for c in range(2):
-            cols = slice(c * width, (c + 1) * width)
-            out = gout_buf[c]
-            total = total + (
-                bf16_dot(out, w_high[:, cols], NT) + bf16_dot(out, w_low[:, cols], NT)
-            )
-        gpart[g] = total.reshape(seqs, piece, HDIM)
-        g_copies(send, g)
-
-    loop(pairs, partial_grad)
+    def rest(step):
+        w_step(step + ahead)
+
+    loop(pairs + len(stages) - ahead, rest)
 
     m_buf[...] = jnp.zeros_like(m_buf)
 
-    def partial_mixed(g):
+    def partial_mixed(step):
+        g = exclusive(step, pair)
         loop(seqs, lambda t: arrived(attn_buf.at[g, t], attn_recv.at[g, t]))
-        a_high, a_low = halves(attn_buf[g].reshape(rows, HDIM))
+        attn = jnp.concatenate(
+            [attn_buf[g, :, a].reshape(STRIDE, HDIM) for a in range(RUNS)], axis=0
+        )
+        a_high, a_low = halves(attn)
         w_high, w_low = halves(head_rows(g))
         for c in range(2):
             cols = slice(c * width, (c + 1) * width)
@@ -337,7 +363,13 @@
     for c in range(2):
         for t in range(seqs):
             arrived(e_buf.at[c, t], e_recv.at[c, t])
-    grads_ref[...] = e_buf[0] + e_buf[1]
+    grads = e_buf[0] + e_buf[1]
+    query_key = jnp.concatenate([grads[:, a].reshape(STRIDE, HDIM) for a in range(RUNS)], axis=0).T
+    grad_query_ref[...] = query_key[:HALF]
+    grad_key_ref[...] = query_key[HALF:]
+    value_pair = grads[:, RUNS].reshape(STRIDE, HDIM).T
+    grad_value_ref[:, :STRIDE] = value_pair[:HALF]
+    grad_value_ref[:, STRIDE:] = value_pair[HALF:]
 
     loop(seqs, functools.partial(pack_copies, sent))
     loop(pairs, functools.partial(w_copies, sent))
@@ -362,37 +394,33 @@
     res = STRIDE // seqs
     pairs = heads // 2
     share = min(seqs, HALF // 8)
-    piece = RUNS * res
-    query_key = jnp.concatenate([queries, keys], axis=1).reshape(RUNS, seqs, res, HDIM)
-    value_pair = jnp.concatenate([values[: rows // 2], values[rows // 2 :]], axis=1)
-    packed = jnp.concatenate([query_key, value_pair.reshape(1, seqs, res, HDIM)], axis=0)
-    packed = packed.transpose(1, 0, 2, 3)
-    cotangent = grad_out.reshape(RUNS, seqs, res, width).transpose(1, 0, 2, 3)
-    cotangent = cotangent.reshape(rows, width)
     vmem = pl.BlockSpec(memory_space=pltpu.VMEM)
     hbm = pl.BlockSpec(memory_space=pl.ANY)
     dma = pltpu.SemaphoreType.DMA
     f32 = jnp.float32
-    mixed, grads = pl.pallas_call(
+    mixed, grad_queries, grad_keys, grad_values = pl.pallas_call(
         functools.partial(kernel, seqs, heads, share),
         out_shape=(
             jax.ShapeDtypeStruct((rows, width), f32),
-            jax.ShapeDtypeStruct((seqs, RUNS + 1, res, HDIM), f32),
+            jax.ShapeDtypeStruct((HALF, rows), f32),
+            jax.ShapeDtypeStruct((HALF, rows), f32),
+            jax.ShapeDtypeStruct((HALF, rows), f32),
         ),
-        in_specs=[pl.BlockSpec(memory_space=pltpu.SMEM), vmem, vmem, hbm, hbm],
-        out_specs=(vmem, vmem),
+        in_specs=[pl.BlockSpec(memory_space=pltpu.SMEM), vmem, vmem, vmem, vmem, hbm, hbm],
+        out_specs=(vmem, vmem, vmem, vmem),
         scratch_shapes=[
             pltpu.VMEM((heads, share, HALF // share, 2 * width), f32),
+            pltpu.VMEM((seqs, RUNS + 1, res, HDIM), f32),
             pltpu.VMEM((2, seqs, RUNS + 1, res, HDIM), f32),
             pltpu.VMEM((2, rows, width), jnp.bfloat16),
             pltpu.VMEM((rows, HDIM), f32),
             pltpu.VMEM((rows, HDIM), f32),
             pltpu.VMEM((seqs, RUNS, res, HDIM), f32),
             pltpu.VMEM((rows, rows), f32),
-            pltpu.VMEM((seqs, piece, HDIM), f32),
-            pltpu.VMEM((pairs, seqs, piece, HDIM), f32),
-            pltpu.VMEM((pairs, seqs, piece, HDIM), f32),
-            pltpu.VMEM((pairs, seqs, piece, HDIM), f32),
+            pltpu.VMEM((seqs, RUNS, res, HDIM), f32),
+            pltpu.VMEM((pairs, seqs, RUNS, res, HDIM), f32),
+            pltpu.VMEM((pairs, seqs, RUNS, res, HDIM), f32),
+            pltpu.VMEM((pairs, seqs, RUNS, res, HDIM), f32),
             pltpu.VMEM((2, rows, width), f32),
             pltpu.VMEM((rows, width), f32),
             pltpu.VMEM((2, seqs, RUNS + 1, res, HDIM), f32),
@@ -414,20 +442,15 @@
             dma((2, seqs)),
         ],
         compiler_params=pltpu.CompilerParams(
-            collective_id=0, has_side_effects=True, vmem_limit_bytes=48 * 1024 * 1024
+            collective_id=0, has_side_effects=True, vmem_limit_bytes=60 * 1024 * 1024
         ),
         cost_estimate=pl.CostEstimate(
             flops=2 * rows * 2 * width * HDIM * pairs * 5,
             bytes_accessed=16 * rows * width,
             transcendentals=rows * rows,
         ),
-    )(local_span, packed, cotangent, wo_local, wo_strided)
-    mixed = mixed.reshape(seqs, RUNS, res, width).transpose(1, 0, 2, 3).reshape(rows, width)
-    grads = grads.transpose(1, 0, 2, 3).reshape(RUNS + 1, rows // RUNS, HDIM)
-    grad_queries = grads[:RUNS, :, :HALF].reshape(rows, HALF)
-    grad_keys = grads[:RUNS, :, HALF:].reshape(rows, HALF)
-    grad_values = jnp.concatenate([grads[RUNS, :, :HALF], grads[RUNS, :, HALF:]], axis=0)
-    return (mixed, grad_queries, grad_keys, grad_values)
+    )(local_span, queries.T, keys.T, values.T, grad_out, wo_local, wo_strided)
+    return (mixed, grad_queries.T, grad_keys.T, grad_values.T)
 
 
 def solution(mesh):

time: 72.6 us -> 69.3 us (0.955)
  local copies, waits for them, and re-layouts: 7.66 us -> 4.26 us
    reshape x3 -> x0, local copies, waits for them, and re-layouts: 2.4 us -> none  [the longest x1 0.97 us: local(): cotangent = grad_out.reshape(RUNS, seqs, res, width).transpose(1, 0, 2, 3)]
    unnamed x9 -> x10, local copies, waits for them, and re-layouts: 3.22 us -> 4.26 us
    slice x2 -> x0, local copies, waits for them, and re-layouts: 1.02 us -> none  [the longest x1 0.93 us: local(): values[:rows // 2]]
    transpose x2 -> x0, local copies, waits for them, and re-layouts: 0.85 us -> none  [the longest x1 0.83 us: local(): mixed.reshape(seqs, RUNS, res, width).transpose(1, 0, 2, 3)]
where the time goes in v2:
time: 69.3 us; the launch traced here: 69 us
  Pallas kernels  64.1 us (92%)
  local copies, waits for them, and re-layouts  4.26 us (6%)
    pallas_call x1, Pallas kernels, local(): pl.pallas_call(functools.partial(kernel, seqs, heads, share), out_shape=(...  64.1 us
    unnamed x10, local copies, waits for them, and re-layouts  4.26 us

profile of v2, /device:TPU:1, one launch (start us, length us, event | category | flops | bytes accessed | tf_op | source)
XLA Modules:
  0.0 69.0 jit_solution(1557976396265611688)
XLA Ops:
  0.6 64.1 %shard_map.102 = (f32[256,512]{1,0:T(8,128)}, f32[64,256]{1,0:T(8,128)}, f32[64,256]{1,0:T(8,128)}, f32[64,256]{1,0:T(8,128)}) custom-call(s32[4]{0:T(128)} %span_ref.1, f32[64,256]{1,0:T(8,128)} %bitcast.9, f32[64,256]{1,0:T(8,128)} %bitcast.10, f32[64,256]{1,0:T(8,128)} %bitcast.11, bf16[256,512]{1,0:T(8,128)(2,1)} %gout_ref.1, f32[64,4096]{1,0:T(8,128)} %wo_local_ref.1, ...), custom_call_target="tpu_custom_call" | custom-call | flops 1342177280 | bytes 2097152 | tf_op jit(solution)/shard_map/pallas_call | solution.py:401
  64.8 0.0 copy-start.2
  64.8 1.9 %copy.15 = f32[256,512]{1,0:T(8,128)} copy(f32[256,512]{1,0:T(8,128)} %get-tuple-element.16) | data formatting | bytes 1048576
  66.7 0.0 copy-done.2
  66.7 0.0 copy-start.1
  66.7 0.6 copy.16
  67.3 0.2 copy-done.1
  67.5 0.0 copy-start
  67.5 0.6 copy.17
  68.2 0.2 copy-done
  68.4 0.6 copy.18
Async XLA Ops:
  64.8 1.9 %copy-start.2 = (f32[64,256]{1,0:T(8,128)S(1)}, f32[64,256]{1,0:T(8,128)}, u32[]{:S(2)}) copy-start(f32[64,256]{1,0:T(8,128)} %get-tuple-element.9) | copy-start | bytes 196612
  66.7 0.9 %copy-start.1 = (f32[64,256]{1,0:T(8,128)S(1)}, f32[64,256]{1,0:T(8,128)}, u32[]{:S(2)}) copy-start(f32[64,256]{1,0:T(8,128)} %get-tuple-element.10) | copy-start | bytes 196612
  67.5 0.9 %copy-start = (f32[64,256]{1,0:T(8,128)S(1)}, f32[64,256]{1,0:T(8,128)}, u32[]{:S(2)}) copy-start(f32[64,256]{1,0:T(8,128)} %get-tuple-element.11) | copy-start | bytes 196612

commit v3 on v2

--- a/solution.py
+++ b/solution.py
@@ -94,13 +94,8 @@
         def _():
             remote(src, dst, send_sem, recv_sem, s, h).start()
 
-    def sent(src, dst, send_sem, recv_sem, s, h):
-        @pl.when(jnp.logical_not(is_me(s, h)))
-        def _():
-            remote(src, dst, send_sem, recv_sem, s, h).wait_send()
-
-    def arrived(dst, recv_sem):
-        pltpu.make_async_copy(dst, dst, recv_sem).wait()
+    def arrived(like, sem):
+        pltpu.make_async_copy(like, like, sem).wait()
 
     def loop(count, body):
         def step(i, carry):
@@ -110,19 +105,23 @@
 
     barrier = pltpu.get_barrier_semaphore()
 
-    def greet(i):
-        s, h = lax.div(i, heads), lax.rem(i, heads)
-        near = jnp.logical_or(s == me_s, lax.div(h, 2) == pair)
-        odd = jnp.logical_and(lax.rem(h, 2) == 1, side == 1)
-        wanted = jnp.logical_or(near, odd)
-
-        @pl.when(jnp.logical_and(wanted, jnp.logical_not(is_me(s, h))))
+    def greet(s, h):
+        pl.semaphore_signal(
+            barrier, inc=1, device_id=(s, h), device_id_type=pl.DeviceIdType.MESH
+        )
+
+    loop(heads - 1, lambda i: greet(me_s, lax.rem(me_h + 1 + i, heads)))
+
+    def greet_seq(i):
+        s = lax.rem(me_s + 1 + i, seqs)
+        greet(s, me_h)
+        greet(s, partner)
+
+        @pl.when(side == 1)
         def _():
-            pl.semaphore_signal(
-                barrier, inc=1, device_id=(s, h), device_id_type=pl.DeviceIdType.MESH
-            )
-
-    loop(seqs * heads, greet)
+            loop(pairs - 1, lambda n: greet(s, lax.rem(me_h + 2 + 2 * n, heads)))
+
+    loop(seqs - 1, greet_seq)
 
     query_key = jnp.concatenate([query_ref[...], key_ref[...]], axis=0).T
     for a in range(RUNS):
@@ -134,28 +133,28 @@
         barrier, heads - 1 + 2 * (seqs - 1) + side * (seqs - 1) * (pairs - 1)
     )
 
-    def pack_copies(act, t):
+    def pack_copies(t):
         for other in range(2):
             s = (1 - other) * me_s + other * t
             slot = (1 - other) * t + other * me_s
-            act(
-                pack_ref.at[t], pack_buf.at[side, slot], pack_send.at[other, t],
-                pack_recv.at[side, slot], s, 2 * pair + other,
-            )
-
-    loop(seqs, functools.partial(pack_copies, send))
-
-    def w_copies(act, step):
+            send(
+                pack_ref.at[t], pack_buf.at[side, slot], pack_send.at[other],
+                pack_recv.at[0], s, 2 * pair + other,
+            )
+
+    loop(seqs, pack_copies)
+
+    def w_copies(step):
         z = exclusive(step, pair)
         own_rows = pl.ds(pl.multiple_of(quarter * w_rows, 8), w_rows)
         cols = pl.ds(pl.multiple_of(z * 2 * width, 128), 2 * width)
         for other, source in ((0, wo_local_ref), (1, wo_strided_ref)):
-            act(
-                source.at[own_rows, cols], w_buf.at[me_h, quarter], w_send.at[z, other],
-                w_recv.at[me_h, quarter], me_s, 2 * z + other,
-            )
-
-    loop(pairs, functools.partial(w_copies, send))
+            send(
+                source.at[own_rows, cols], w_buf.at[me_h, quarter], w_send.at[0],
+                w_recv.at[pair, quarter], me_s, 2 * z + other,
+            )
+
+    loop(pairs, w_copies)
 
     gout_copy = remote(
         gout_ref, gout_buf.at[side], gout_send.at[0], gout_recv.at[0], me_s, partner
@@ -163,22 +162,18 @@
     gout_copy.start()
     gout_buf[side] = gout_ref[...]
 
-    def share_copy(act, j, stage, offset_at, offset, distance):
+    def row_part(offset):
         q = quarter
         for bit in (1, 2, 4, 8, 16, 32):
             if offset & bit:
                 q = flip(q, bit)
-        act(
-            w_buf.at[j, q], w_buf.at[j, q], share_send.at[j, stage + offset_at],
-            w_recv.at[j, q], flip(me_s, distance), me_h,
-        )
-
-    def w_arrived(j, offset):
-        q = quarter
-        for bit in (1, 2, 4, 8, 16, 32):
-            if offset & bit:
-                q = flip(q, bit)
-        arrived(w_buf.at[j, q], w_recv.at[j, q])
+        return q
+
+    def w_part(z, offset):
+        return w_buf.at[pl.ds(2 * z, 2), row_part(offset)]
+
+    def w_arrived(z, offset):
+        arrived(w_part(z, offset), w_recv.at[z, row_part(offset)])
 
     stages, held, fresh, distance = [], [0], [0], share // 2
     while distance:
@@ -189,30 +184,32 @@
 
     def run_stage(at, z):
         distance, held_here, fresh_here = stages[at]
-        first = sum(len(s[1]) for s in stages[:at])
-        for c in range(2):
-            j = 2 * z + c
-            for n, offset in enumerate(held_here):
-                if offset in fresh_here:
-                    w_arrived(j, offset)
-                share_copy(send, j, first, n, offset, distance)
+        for offset in held_here:
+            if offset in fresh_here:
+                w_arrived(z, offset)
+            remote(
+                w_part(z, offset), w_part(z, offset), share_send.at[at],
+                w_recv.at[z, row_part(offset)], flip(me_s, distance), me_h,
+            ).start()
 
     def head_rows(g):
         return w_buf[pl.ds(2 * g, 2)].reshape(HDIM, 2 * width)
 
-    def g_copies(act, g):
+    def own_or_other(sems, z):
+        return sems.at[jnp.where(z == pair, 1, 0)]
+
+    def g_copies(g):
         def one(t):
-            act(
-                gpart.at[g, t], g_buf.at[pair, to_slot(t)], g_send.at[g, t],
-                g_recv.at[pair, to_slot(t)], to_seq(t), 2 * g + side,
+            send(
+                gpart.at[g, t], g_buf.at[pair, to_slot(t)], own_or_other(g_send, g),
+                g_recv.at[0], to_seq(t), 2 * g + side,
             )
 
         loop(seqs, one)
 
     def partial_grad(g):
         for offset in fresh:
-            for c in range(2):
-                w_arrived(2 * g + c, offset)
+            w_arrived(g, offset)
         w_high, w_low = halves(head_rows(g))
         total = jnp.zeros((rows, HDIM), jnp.float32)
         for c in range(2):
@@ -223,11 +220,11 @@
             )
         for a in range(RUNS):
             gpart[g, :, a] = total[a * STRIDE : (a + 1) * STRIDE].reshape(seqs, res, HDIM)
-        g_copies(send, g)
+        g_copies(g)
 
     def w_step(step):
         for at in range(len(stages) + 1):
-            turn_of = step - at
+            turn_of = step - at - at // len(stages)
 
             @pl.when(jnp.logical_and(turn_of >= 0, turn_of < pairs))
             def _(at=at, turn_of=turn_of):
@@ -237,13 +234,11 @@
                 else:
                     partial_grad(z)
 
-    ahead = min(2, len(stages))
+    ahead = 2
 
     loop(ahead, w_step)
 
-    for c in range(2):
-        for t in range(seqs):
-            arrived(pack_buf.at[c, t], pack_recv.at[c, t])
+    arrived(pack_buf, pack_recv.at[0])
 
     lane = lax.broadcasted_iota(jnp.int32, (rows, HDIM), 1) < HALF
     lane_half = lax.broadcasted_iota(jnp.int32, (rows // 2, HDIM), 1) < HALF
@@ -284,26 +279,27 @@
     weights = jnp.where(allowed, jnp.exp(scores - row_max), 0.0)
     probs = weights / jnp.sum(weights, axis=-1, keepdims=True)
     p_buf[...] = probs
+    w_step(ahead)
     attended = exact_dot(probs, v_buf[...].reshape(rows, HDIM), NN)
     attn_own[...] = attended.reshape(seqs, RUNS, res, HDIM)
 
-    def attn_copies(act, step):
+    def attn_copies(step):
         z = exclusive(step, pair)
 
         def one(t):
-            act(
-                attn_own.at[t], attn_buf.at[pair, to_slot(t)], attn_send.at[z, t],
-                attn_recv.at[pair, to_slot(t)], to_seq(t), 2 * z + side,
+            send(
+                attn_own.at[t], attn_buf.at[pair, to_slot(t)], own_or_other(attn_send, z),
+                attn_recv.at[pair], to_seq(t), 2 * z + side,
             )
 
         loop(seqs, one)
 
-    loop(pairs, functools.partial(attn_copies, send))
+    loop(pairs, attn_copies)
 
     gout_copy.wait_recv()
 
     def rest(step):
-        w_step(step + ahead)
+        w_step(step + ahead + 1)
 
     loop(pairs + len(stages) - ahead, rest)
 
@@ -311,7 +307,7 @@
 
     def partial_mixed(step):
         g = exclusive(step, pair)
-        loop(seqs, lambda t: arrived(attn_buf.at[g, t], attn_recv.at[g, t]))
+        arrived(attn_buf.at[g], attn_recv.at[g])
         attn = jnp.concatenate(
             [attn_buf[g, :, a].reshape(STRIDE, HDIM) for a in range(RUNS)], axis=0
         )
@@ -329,10 +325,7 @@
     )
     m_copy.start()
 
-    def g_arrived(z):
-        loop(seqs, lambda t: arrived(g_buf.at[z, t], g_recv.at[z, t]))
-
-    loop(pairs, g_arrived)
+    arrived(g_buf, g_recv.at[0])
     incoming = jnp.sum(g_buf[...], axis=0).reshape(rows, HDIM)
     delta = jnp.sum(incoming * attn_own[...].reshape(rows, HDIM), axis=-1, keepdims=True)
     dprobs = exact_dot(incoming, v_buf[...].reshape(rows, HDIM), NT)
@@ -348,21 +341,33 @@
     e_out[0, :, RUNS] = jnp.where(lane_half, dv_first, turn(dv_second)).reshape(seqs, res, HDIM)
     e_out[1, :, RUNS] = jnp.where(lane_half, turn(dv_first), dv_second).reshape(seqs, res, HDIM)
 
-    def e_copies(act, t):
+    def e_copies(t):
         for c in range(2):
-            act(
-                e_out.at[c, t], e_buf.at[side, to_slot(t)], e_send.at[c, t],
-                e_recv.at[side, to_slot(t)], to_seq(t), 2 * pair + c,
-            )
-
-    loop(seqs, functools.partial(e_copies, send))
+            send(
+                e_out.at[c, t], e_buf.at[side, to_slot(t)], e_send.at[c],
+                e_recv.at[0], to_seq(t), 2 * pair + c,
+            )
+
+    loop(seqs, e_copies)
+
+    arrived(pack_ref, pack_send.at[1 - side])
+    arrived(w_buf.at[pl.ds(0, heads - 1), 0], w_send.at[0])
+    gout_copy.wait_send()
+    for at, (_, held_here, _) in enumerate(stages):
+        arrived(w_buf.at[:, pl.ds(0, len(held_here))], share_send.at[at])
+    arrived(attn_buf.at[pl.ds(0, pairs - 1)], attn_send.at[0])
+    arrived(gpart.at[pl.ds(0, pairs - 1)], g_send.at[0])
+
+    @pl.when(side == 1)
+    def _():
+        arrived(pack_ref.at[pl.ds(0, seqs - 1)], pack_send.at[1])
+        arrived(attn_own.at[pl.ds(0, seqs - 1)], attn_send.at[1])
+        arrived(attn_own.at[pl.ds(0, seqs - 1)], g_send.at[1])
 
     m_copy.wait_recv()
     mixed_ref[...] = m_buf[side] + m_recv[...]
 
-    for c in range(2):
-        for t in range(seqs):
-            arrived(e_buf.at[c, t], e_recv.at[c, t])
+    arrived(e_buf, e_recv.at[0])
     grads = e_buf[0] + e_buf[1]
     query_key = jnp.concatenate([grads[:, a].reshape(STRIDE, HDIM) for a in range(RUNS)], axis=0).T
     grad_query_ref[...] = query_key[:HALF]
@@ -371,21 +376,22 @@
     grad_value_ref[:, :STRIDE] = value_pair[:HALF]
     grad_value_ref[:, STRIDE:] = value_pair[HALF:]
 
-    loop(seqs, functools.partial(pack_copies, sent))
-    loop(pairs, functools.partial(w_copies, sent))
-    gout_copy.wait_send()
-    first = 0
-    for distance, held_here, _ in stages:
-        def left(j, distance=distance, held_here=held_here, first=first):
-            for n, offset in enumerate(held_here):
-                share_copy(sent, j, first, n, offset, distance)
-
-        loop(heads, left)
-        first += len(held_here)
-    loop(pairs, functools.partial(attn_copies, sent))
-    loop(pairs, functools.partial(g_copies, sent))
     m_copy.wait_send()
-    loop(seqs, functools.partial(e_copies, sent))
+    arrived(e_out.at[0], e_send.at[1 - side])
+
+    @pl.when(side == 1)
+    def _():
+        arrived(e_out.at[0, pl.ds(0, seqs - 1)], e_send.at[1])
+
+
+def write_kernel(*refs):
+    count = len(refs) // 2
+    sems = refs[-1]
+    copies = [pltpu.make_async_copy(refs[i], refs[count + i], sems.at[i]) for i in range(count)]
+    for copy in copies:
+        copy.start()
+    for copy in copies:
+        copy.wait()
 
 
 def local(queries, keys, values, local_span, wo_local, wo_strided, grad_out):
@@ -395,10 +401,10 @@
     pairs = heads // 2
     share = min(seqs, HALF // 8)
     vmem = pl.BlockSpec(memory_space=pltpu.VMEM)
-    hbm = pl.BlockSpec(memory_space=pl.ANY)
+    hbm = pl.BlockSpec(memory_space=pltpu.HBM)
     dma = pltpu.SemaphoreType.DMA
     f32 = jnp.float32
-    mixed, grad_queries, grad_keys, grad_values = pl.pallas_call(
+    results = pl.pallas_call(
         functools.partial(kernel, seqs, heads, share),
         out_shape=(
             jax.ShapeDtypeStruct((rows, width), f32),
@@ -425,24 +431,24 @@
             pltpu.VMEM((rows, width), f32),
             pltpu.VMEM((2, seqs, RUNS + 1, res, HDIM), f32),
             pltpu.VMEM((2, seqs, RUNS + 1, res, HDIM), f32),
-            dma((pairs, 2)),
-            dma((heads, share)),
-            dma((heads, share)),
-            dma((2, seqs)),
-            dma((2, seqs)),
-            dma((1,)),
-            dma((1,)),
-            dma((pairs, seqs)),
-            dma((pairs, seqs)),
-            dma((pairs, seqs)),
-            dma((pairs, seqs)),
-            dma((1,)),
-            dma((1,)),
-            dma((2, seqs)),
-            dma((2, seqs)),
+            dma((1,)),
+            dma((pairs, share)),
+            dma((max(1, share.bit_length() - 1),)),
+            dma((2,)),
+            dma((1,)),
+            dma((1,)),
+            dma((1,)),
+            dma((2,)),
+            dma((pairs,)),
+            dma((2,)),
+            dma((1,)),
+            dma((1,)),
+            dma((1,)),
+            dma((2,)),
+            dma((1,)),
         ],
         compiler_params=pltpu.CompilerParams(
-            collective_id=0, has_side_effects=True, vmem_limit_bytes=60 * 1024 * 1024
+            collective_id=0, has_side_effects=True, vmem_limit_bytes=48 * 1024 * 1024
         ),
         cost_estimate=pl.CostEstimate(
             flops=2 * rows * 2 * width * HDIM * pairs * 5,
@@ -450,6 +456,14 @@
             transcendentals=rows * rows,
         ),
     )(local_span, queries.T, keys.T, values.T, grad_out, wo_local, wo_strided)
+    anywhere = pl.BlockSpec(memory_space=pl.ANY)
+    mixed, grad_queries, grad_keys, grad_values = pl.pallas_call(
+        write_kernel,
+        out_shape=[jax.ShapeDtypeStruct(x.shape, x.dtype) for x in results],
+        in_specs=[anywhere] * len(results),
+        out_specs=[hbm] * len(results),
+        scratch_shapes=[dma((len(results),))],
+    )(*results)
     return (mixed, grad_queries.T, grad_keys.T, grad_values.T)
 
 

time: 69.3 us -> 90.7 us (1.31)
  Pallas kernels: 64.1 us -> 80.3 us
  local copies, waits for them, and re-layouts: 4.26 us -> 9.24 us
    pallas_call x0 -> x1, Pallas kernels: none -> 23 us  [local(): pl.pallas_call(write_kernel, out_shape=[jax.ShapeDtypeStruct(x.shape, x.d...]
    pallas_call x1, Pallas kernels: 64.1 us -> 57.4 us  [local(): pl.pallas_call(functools.partial(kernel, seqs, heads, share), out_shape=(...]
    unnamed x10 -> x22, local copies, waits for them, and re-layouts: 4.26 us -> 9.24 us
where the time goes in v3:
time: 90.7 us; the launch traced here: 90.3 us
  Pallas kernels  80.3 us (89%)
  local copies, waits for them, and re-layouts  9.24 us (10%)
    pallas_call x1, Pallas kernels, local(): pl.pallas_call(functools.partial(kernel, seqs, heads, share), out_shape=(...  57.4 us
    pallas_call x1, Pallas kernels, local(): pl.pallas_call(write_kernel, out_shape=[jax.ShapeDtypeStruct(x.shape, x.d...  23 us
    unnamed x22, local copies, waits for them, and re-layouts  9.24 us

profile of v3, /device:TPU:1, one launch (start us, length us, event | category | flops | bytes accessed | tf_op | source)
XLA Modules:
  0.0 90.3 jit_solution(1506132494009080322)
XLA Ops:
  0.6 0.0 copy-start.10
  0.6 0.6 copy-done.10
  1.3 0.0 copy-start.4
  1.3 1.2 %copy-done.4 = f32[64,4096]{1,0:T(8,128)S(1)} copy-done((f32[64,4096]{1,0:T(8,128)S(1)}, f32[64,4096]{1,0:T(8,128)}, u32[]{:S(2)}) %copy-start.4) | copy-done | bytes 1048600
  2.5 0.0 copy-start.5
  2.5 1.2 %copy-done.5 = f32[64,4096]{1,0:T(8,128)S(1)} copy-done((f32[64,4096]{1,0:T(8,128)S(1)}, f32[64,4096]{1,0:T(8,128)}, u32[]{:S(2)}) %copy-start.5) | copy-done | bytes 1048600
  3.7 0.0 copy-start.6
  3.7 0.9 %copy-done.6 = bf16[256,512]{1,0:T(8,128)(2,1)S(1)} copy-done((bf16[256,512]{1,0:T(8,128)(2,1)S(1)}, bf16[256,512]{1,0:T(8,128)(2,1)}, u32[]{:S(2)}) %copy-start.6) | copy-done | bytes 262168
  4.7 0.0 copy-start.7
  4.7 0.8 copy-done.7
  5.5 0.0 copy-start.8
  5.5 0.8 copy-done.8
  6.4 0.0 copy-start.9
  6.4 0.8 copy-done.9
  7.2 57.4 %shard_map.102 = (f32[256,512]{1,0:T(8,128)S(1)}, f32[64,256]{1,0:T(8,128)S(1)}, f32[64,256]{1,0:T(8,128)S(1)}, f32[64,256]{1,0:T(8,128)S(1)}) custom-call(s32[4]{0:T(128)S(1)} %copy-done.10, f32[64,256]{1,0:T(8,128)S(1)} %bitcast.6, f32[64,256]{1,0:T(8,128)S(1)} %bitcast.7, f32[64,256]{1,0:T(8,128)S(1)} %bitcast.8, bf16[256,512]{1,0:T(8,128)(2,1)S(1)} %copy-done.6, ...), custom_call_target="tpu_custom_call" | custom-call | flops 1342177280 | bytes 2097152 | tf_op jit(solution)/shard_map/pallas_call | solution.py:407
  64.6 0.0 copy-start
  64.6 0.8 copy-done
  65.4 0.0 copy-start.1
  65.4 0.6 copy-done.1
  66.0 0.0 copy-start.2
  66.0 0.6 copy-done.2
  66.7 0.0 copy-start.3
  66.7 0.6 copy-done.3
  67.3 23.0 %shard_map.103 = (f32[256,512]{1,0:T(8,128)}, f32[64,256]{1,0:T(8,128)}, f32[64,256]{1,0:T(8,128)}, f32[64,256]{1,0:T(8,128)}) custom-call(f32[256,512]{1,0:T(8,128)} %copy-done, f32[64,256]{1,0:T(8,128)} %copy-done.1, f32[64,256]{1,0:T(8,128)} %copy-done.2, f32[64,256]{1,0:T(8,128)} %copy-done.3), custom_call_target="tpu_custom_call" | custom-call | tf_op jit(solution)/shard_map/pallas_call | solution.py:460
Async XLA Ops:
  0.6 0.7 copy-start.10
  1.3 1.2 %copy-start.4 = (f32[64,4096]{1,0:T(8,128)S(1)}, f32[64,4096]{1,0:T(8,128)}, u32[]{:S(2)}) copy-start(f32[64,4096]{1,0:T(8,128)} %wo_local_ref.1) | copy-start | bytes 3145732
  2.5 1.2 %copy-start.5 = (f32[64,4096]{1,0:T(8,128)S(1)}, f32[64,4096]{1,0:T(8,128)}, u32[]{:S(2)}) copy-start(f32[64,4096]{1,0:T(8,128)} %wo_strided_ref.1) | copy-start | bytes 3145732
  3.7 0.9 %copy-start.6 = (bf16[256,512]{1,0:T(8,128)(2,1)S(1)}, bf16[256,512]{1,0:T(8,128)(2,1)}, u32[]{:S(2)}) copy-start(bf16[256,512]{1,0:T(8,128)(2,1)} %gout_ref.1) | copy-start | bytes 786436
  4.7 0.8 copy-start.7
  5.5 0.8 copy-start.8
  6.4 0.8 copy-start.9
  64.6 0.8 copy-start
  65.4 0.6 copy-start.1
  66.0 0.6 copy-start.2
  66.7 0.6 copy-start.3

commit v4 on v3

--- a/solution.py
+++ b/solution.py
@@ -41,10 +41,10 @@
     seqs, heads, share,
     span_ref, query_ref, key_ref, value_ref, gout_ref, wo_local_ref, wo_strided_ref,
     mixed_ref, grad_query_ref, grad_key_ref, grad_value_ref,
-    w_buf, pack_ref, pack_buf, gout_buf, q_buf, k_buf, v_buf, p_buf, attn_own, attn_buf,
-    gpart, g_buf, m_buf, m_recv, e_out, e_buf,
-    w_send, w_recv, share_send, pack_send, pack_recv, gout_send, gout_recv,
-    attn_send, attn_recv, g_send, g_recv, m_send, m_recv_sem, e_send, e_recv,
+    in_buf, w_buf, pack_ref, pack_buf, gout_buf, q_buf, k_buf, v_buf, p_buf, attn_own, attn_buf,
+    gpart, near_buf, g_buf, m_buf, m_recv, e_out, e_buf,
+    in_sem, w_send, w_recv, share_send, pack_send, pack_recv, gout_send, gout_recv,
+    attn_send, attn_recv, hand_send, near_send, near_recv, g_send, g_recv, m_send, m_recv_sem, e_send, e_recv,
 ):
     pairs = heads // 2
     res = STRIDE // seqs
@@ -103,6 +103,14 @@
             return carry
         lax.fori_loop(0, count, step, 0)
 
+    own_inputs = [
+        pltpu.make_async_copy(ref, in_buf.at[i], in_sem.at[i])
+        for i, ref in enumerate((query_ref, key_ref, value_ref))
+    ]
+    own_inputs.append(pltpu.make_async_copy(gout_ref, gout_buf.at[side], in_sem.at[3]))
+    for copy in own_inputs:
+        copy.start()
+
     barrier = pltpu.get_barrier_semaphore()
 
     def greet(s, h):
@@ -123,10 +131,12 @@
 
     loop(seqs - 1, greet_seq)
 
-    query_key = jnp.concatenate([query_ref[...], key_ref[...]], axis=0).T
+    for copy in own_inputs[:3]:
+        copy.wait()
+    query_key = in_buf[:2].reshape(HDIM, rows).T
     for a in range(RUNS):
         pack_ref[:, a] = query_key[a * STRIDE : (a + 1) * STRIDE].reshape(seqs, res, HDIM)
-    value_pair = jnp.concatenate([value_ref[:, :STRIDE], value_ref[:, STRIDE:]], axis=0).T
+    value_pair = jnp.concatenate([in_buf[2, :, :STRIDE], in_buf[2, :, STRIDE:]], axis=0).T
     pack_ref[:, RUNS] = value_pair.reshape(seqs, res, HDIM)
 
     pl.semaphore_wait(
@@ -144,8 +154,13 @@
 
     loop(seqs, pack_copies)
 
+    def gray(step):
+        return exclusive(step, lax.div(step, 2))
+
+    neighbour = exclusive(1, pair)
+
     def w_copies(step):
-        z = exclusive(step, pair)
+        z = exclusive(gray(step), pair)
         own_rows = pl.ds(pl.multiple_of(quarter * w_rows, 8), w_rows)
         cols = pl.ds(pl.multiple_of(z * 2 * width, 128), 2 * width)
         for other, source in ((0, wo_local_ref), (1, wo_strided_ref)):
@@ -160,7 +175,6 @@
         gout_ref, gout_buf.at[side], gout_send.at[0], gout_recv.at[0], me_s, partner
     )
     gout_copy.start()
-    gout_buf[side] = gout_ref[...]
 
     def row_part(offset):
         q = quarter
@@ -198,16 +212,21 @@
     def own_or_other(sems, z):
         return sems.at[jnp.where(z == pair, 1, 0)]
 
-    def g_copies(g):
+    def g_copies(i):
+        g = exclusive(2 * i, pair)
+        arrived(near_buf.at[i], near_recv.at[i])
+        gpart[g] += near_buf[i]
+
         def one(t):
             send(
-                gpart.at[g, t], g_buf.at[pair, to_slot(t)], own_or_other(g_send, g),
+                gpart.at[g, t], g_buf.at[i, to_slot(t)], own_or_other(g_send, g),
                 g_recv.at[0], to_seq(t), 2 * g + side,
             )
 
         loop(seqs, one)
 
-    def partial_grad(g):
+    def partial_grad(k):
+        g = exclusive(k, pair)
         for offset in fresh:
             w_arrived(g, offset)
         w_high, w_low = halves(head_rows(g))
@@ -220,7 +239,14 @@
             )
         for a in range(RUNS):
             gpart[g, :, a] = total[a * STRIDE : (a + 1) * STRIDE].reshape(seqs, res, HDIM)
-        g_copies(g)
+
+        @pl.when(lax.rem(k, 2) == 1)
+        def _():
+            i = lax.div(k, 2)
+            remote(
+                gpart.at[g], near_buf.at[i], near_send.at[0], near_recv.at[i],
+                me_s, 2 * neighbour + side,
+            ).start()
 
     def w_step(step):
         for at in range(len(stages) + 1):
@@ -228,11 +254,11 @@
 
             @pl.when(jnp.logical_and(turn_of >= 0, turn_of < pairs))
             def _(at=at, turn_of=turn_of):
-                z = exclusive(turn_of, pair)
+                k = gray(turn_of)
                 if at < len(stages):
-                    run_stage(at, z)
+                    run_stage(at, exclusive(k, pair))
                 else:
-                    partial_grad(z)
+                    partial_grad(k)
 
     ahead = 2
 
@@ -283,8 +309,8 @@
     attended = exact_dot(probs, v_buf[...].reshape(rows, HDIM), NN)
     attn_own[...] = attended.reshape(seqs, RUNS, res, HDIM)
 
-    def attn_copies(step):
-        z = exclusive(step, pair)
+    def attn_copies(i):
+        z = exclusive(2 * i, pair)
 
         def one(t):
             send(
@@ -294,8 +320,9 @@
 
         loop(seqs, one)
 
-    loop(pairs, attn_copies)
-
+    loop(pairs // 2, attn_copies)
+
+    own_inputs[3].wait()
     gout_copy.wait_recv()
 
     def rest(step):
@@ -303,11 +330,28 @@
 
     loop(pairs + len(stages) - ahead, rest)
 
+    def hand_on(i):
+        g = exclusive(2 * i, pair)
+        arrived(attn_buf.at[g], attn_recv.at[g])
+        remote(
+            attn_buf.at[g], attn_buf.at[g], hand_send.at[0], attn_recv.at[g],
+            me_s, 2 * neighbour + side,
+        ).start()
+
+    loop(pairs // 2, hand_on)
+    loop(pairs // 2, g_copies)
+
     m_buf[...] = jnp.zeros_like(m_buf)
 
     def partial_mixed(step):
-        g = exclusive(step, pair)
-        arrived(attn_buf.at[g], attn_recv.at[g])
+        handed = lax.div(2 * step, pairs)
+        k = 2 * (step - handed * (pairs // 2)) + handed
+        g = exclusive(k, pair)
+
+        @pl.when(handed == 1)
+        def _():
+            arrived(attn_buf.at[g], attn_recv.at[g])
+
         attn = jnp.concatenate(
             [attn_buf[g, :, a].reshape(STRIDE, HDIM) for a in range(RUNS)], axis=0
         )
@@ -355,8 +399,10 @@
     gout_copy.wait_send()
     for at, (_, held_here, _) in enumerate(stages):
         arrived(w_buf.at[:, pl.ds(0, len(held_here))], share_send.at[at])
-    arrived(attn_buf.at[pl.ds(0, pairs - 1)], attn_send.at[0])
-    arrived(gpart.at[pl.ds(0, pairs - 1)], g_send.at[0])
+    arrived(attn_buf.at[pl.ds(0, pairs // 2 - 1)], attn_send.at[0])
+    arrived(attn_buf.at[pl.ds(0, pairs // 2)], hand_send.at[0])
+    arrived(near_buf, near_send.at[0])
+    arrived(gpart.at[pl.ds(0, pairs // 2 - 1)], g_send.at[0])
 
     @pl.when(side == 1)
     def _():
@@ -386,12 +432,8 @@
 
 def write_kernel(*refs):
     count = len(refs) // 2
-    sems = refs[-1]
-    copies = [pltpu.make_async_copy(refs[i], refs[count + i], sems.at[i]) for i in range(count)]
-    for copy in copies:
-        copy.start()
-    for copy in copies:
-        copy.wait()
+    for i in range(count):
+        refs[count + i][...] = refs[i][...]
 
 
 def local(queries, keys, values, local_span, wo_local, wo_strided, grad_out):
@@ -412,9 +454,10 @@
             jax.ShapeDtypeStruct((HALF, rows), f32),
             jax.ShapeDtypeStruct((HALF, rows), f32),
         ),
-        in_specs=[pl.BlockSpec(memory_space=pltpu.SMEM), vmem, vmem, vmem, vmem, hbm, hbm],
+        in_specs=[pl.BlockSpec(memory_space=pltpu.SMEM)] + [hbm] * 6,
         out_specs=(vmem, vmem, vmem, vmem),
         scratch_shapes=[
+            pltpu.VMEM((3, HALF, rows), f32),
             pltpu.VMEM((heads, share, HALF // share, 2 * width), f32),
             pltpu.VMEM((seqs, RUNS + 1, res, HDIM), f32),
             pltpu.VMEM((2, seqs, RUNS + 1, res, HDIM), f32),
@@ -426,11 +469,13 @@
             pltpu.VMEM((seqs, RUNS, res, HDIM), f32),
             pltpu.VMEM((pairs, seqs, RUNS, res, HDIM), f32),
             pltpu.VMEM((pairs, seqs, RUNS, res, HDIM), f32),
-            pltpu.VMEM((pairs, seqs, RUNS, res, HDIM), f32),
+            pltpu.VMEM((pairs // 2, seqs, RUNS, res, HDIM), f32),
+            pltpu.VMEM((pairs // 2, seqs, RUNS, res, HDIM), f32),
             pltpu.VMEM((2, rows, width), f32),
             pltpu.VMEM((rows, width), f32),
             pltpu.VMEM((2, seqs, RUNS + 1, res, HDIM), f32),
             pltpu.VMEM((2, seqs, RUNS + 1, res, HDIM), f32),
+            dma((4,)),
             dma((1,)),
             dma((pairs, share)),
             dma((max(1, share.bit_length() - 1),)),
@@ -440,6 +485,9 @@
             dma((1,)),
             dma((2,)),
             dma((pairs,)),
+            dma((1,)),
+            dma((1,)),
+            dma((pairs // 2,)),
             dma((2,)),
             dma((1,)),
             dma((1,)),
@@ -448,7 +496,7 @@
             dma((1,)),
         ],
         compiler_params=pltpu.CompilerParams(
-            collective_id=0, has_side_effects=True, vmem_limit_bytes=48 * 1024 * 1024
+            collective_id=0, has_side_effects=True, vmem_limit_bytes=60 * 1024 * 1024
         ),
         cost_estimate=pl.CostEstimate(
             flops=2 * rows * 2 * width * HDIM * pairs * 5,
@@ -456,13 +504,12 @@
             transcendentals=rows * rows,
         ),
     )(local_span, queries.T, keys.T, values.T, grad_out, wo_local, wo_strided)
-    anywhere = pl.BlockSpec(memory_space=pl.ANY)
     mixed, grad_queries, grad_keys, grad_values = pl.pallas_call(
         write_kernel,
         out_shape=[jax.ShapeDtypeStruct(x.shape, x.dtype) for x in results],
-        in_specs=[anywhere] * len(results),
-        out_specs=[hbm] * len(results),
-        scratch_shapes=[dma((len(results),))],
+        in_specs=[vmem] * len(results),
+        out_specs=[vmem] * len(results),
+        compiler_params=pltpu.CompilerParams(vmem_limit_bytes=60 * 1024 * 1024),
     )(*results)
     return (mixed, grad_queries.T, grad_keys.T, grad_values.T)
 

time: 90.7 us -> 68.5 us (0.76)
  Pallas kernels: 80.3 us -> 67.6 us
  local copies, waits for them, and re-layouts: 9.24 us -> 0 us
    pallas_call x1, Pallas kernels: 23 us -> 1.95 us  [local(): pl.pallas_call(write_kernel, out_shape=[jax.ShapeDtypeStruct(x.shape, x.d...]
    unnamed x22 -> x0, local copies, waits for them, and re-layouts: 9.24 us -> none
    pallas_call x1, Pallas kernels: 57.4 us -> 65.6 us  [local(): pl.pallas_call(functools.partial(kernel, seqs, heads, share), out_shape=(...]
where the time goes in v4:
time: 68.5 us; the launch traced here: 68.2 us
  Pallas kernels  67.6 us (99%)
    pallas_call x1, Pallas kernels, local(): pl.pallas_call(functools.partial(kernel, seqs, heads, share), out_shape=(...  65.6 us
    pallas_call x1, Pallas kernels, local(): pl.pallas_call(write_kernel, out_shape=[jax.ShapeDtypeStruct(x.shape, x.d...  1.95 us

profile of v4, /device:TPU:1, one launch (start us, length us, event | category | flops | bytes accessed | tf_op | source)
XLA Modules:
  0.0 68.2 jit_solution(1869102640273599528)
XLA Ops:
  0.6 65.6 %shard_map.102 = (f32[256,512]{1,0:T(8,128)}, f32[64,256]{1,0:T(8,128)}, f32[64,256]{1,0:T(8,128)}, f32[64,256]{1,0:T(8,128)}) custom-call(s32[4]{0:T(128)} %span_ref.1, f32[64,256]{1,0:T(8,128)} %bitcast.6, f32[64,256]{1,0:T(8,128)} %bitcast.7, f32[64,256]{1,0:T(8,128)} %bitcast.8, bf16[256,512]{1,0:T(8,128)(2,1)} %gout_ref.1, f32[64,4096]{1,0:T(8,128)} %wo_local_ref.1, ...), custom_call_target="tpu_custom_call" | custom-call | flops 1342177280 | bytes 2097152 | tf_op jit(solution)/shard_map/pallas_call | solution.py:449
  66.3 1.9 %shard_map.103 = (f32[256,512]{1,0:T(8,128)}, f32[64,256]{1,0:T(8,128)}, f32[64,256]{1,0:T(8,128)}, f32[64,256]{1,0:T(8,128)}) custom-call(f32[256,512]{1,0:T(8,128)} %get-tuple-element.12.refs_0_, f32[64,256]{1,0:T(8,128)} %get-tuple-element.13.refs_1_, f32[64,256]{1,0:T(8,128)} %get-tuple-element.14.refs_2_, f32[64,256]{1,0:T(8,128)} %get-tuple-element.15.refs_3_), custom_call_target="tpu_custom_call" | custom-call | tf_op jit(solution)/shard_map/pallas_call | solution.py:507

commit v5 on v3

--- a/solution.py
+++ b/solution.py
@@ -41,9 +41,9 @@
     seqs, heads, share,
     span_ref, query_ref, key_ref, value_ref, gout_ref, wo_local_ref, wo_strided_ref,
     mixed_ref, grad_query_ref, grad_key_ref, grad_value_ref,
-    w_buf, pack_ref, pack_buf, gout_buf, q_buf, k_buf, v_buf, p_buf, attn_own, attn_buf,
+    in_buf, w_buf, pack_ref, pack_buf, gout_buf, q_buf, k_buf, v_buf, p_buf, attn_own, attn_buf,
     gpart, g_buf, m_buf, m_recv, e_out, e_buf,
-    w_send, w_recv, share_send, pack_send, pack_recv, gout_send, gout_recv,
+    in_sem, w_send, w_recv, share_send, pack_send, pack_recv, gout_send, gout_recv,
     attn_send, attn_recv, g_send, g_recv, m_send, m_recv_sem, e_send, e_recv,
 ):
     pairs = heads // 2
@@ -103,6 +103,14 @@
             return carry
         lax.fori_loop(0, count, step, 0)
 
+    own_inputs = [
+        pltpu.make_async_copy(ref, in_buf.at[i], in_sem.at[i])
+        for i, ref in enumerate((query_ref, key_ref, value_ref))
+    ]
+    own_inputs.append(pltpu.make_async_copy(gout_ref, gout_buf.at[side], in_sem.at[3]))
+    for copy in own_inputs:
+        copy.start()
+
     barrier = pltpu.get_barrier_semaphore()
 
     def greet(s, h):
@@ -123,26 +131,9 @@
 
     loop(seqs - 1, greet_seq)
 
-    query_key = jnp.concatenate([query_ref[...], key_ref[...]], axis=0).T
-    for a in range(RUNS):
-        pack_ref[:, a] = query_key[a * STRIDE : (a + 1) * STRIDE].reshape(seqs, res, HDIM)
-    value_pair = jnp.concatenate([value_ref[:, :STRIDE], value_ref[:, STRIDE:]], axis=0).T
-    pack_ref[:, RUNS] = value_pair.reshape(seqs, res, HDIM)
-
     pl.semaphore_wait(
         barrier, heads - 1 + 2 * (seqs - 1) + side * (seqs - 1) * (pairs - 1)
     )
-
-    def pack_copies(t):
-        for other in range(2):
-            s = (1 - other) * me_s + other * t
-            slot = (1 - other) * t + other * me_s
-            send(
-                pack_ref.at[t], pack_buf.at[side, slot], pack_send.at[other],
-                pack_recv.at[0], s, 2 * pair + other,
-            )
-
-    loop(seqs, pack_copies)
 
     def w_copies(step):
         z = exclusive(step, pair)
@@ -156,11 +147,29 @@
 
     loop(pairs, w_copies)
 
+    for copy in own_inputs[:3]:
+        copy.wait()
+    query_key = in_buf[:2].reshape(HDIM, rows).T
+    for a in range(RUNS):
+        pack_ref[:, a] = query_key[a * STRIDE : (a + 1) * STRIDE].reshape(seqs, res, HDIM)
+    value_pair = jnp.concatenate([in_buf[2, :, :STRIDE], in_buf[2, :, STRIDE:]], axis=0).T
+    pack_ref[:, RUNS] = value_pair.reshape(seqs, res, HDIM)
+
+    def pack_copies(t):
+        for other in range(2):
+            s = (1 - other) * me_s + other * t
+            slot = (1 - other) * t + other * me_s
+            send(
+                pack_ref.at[t], pack_buf.at[side, slot], pack_send.at[other],
+                pack_recv.at[0], s, 2 * pair + other,
+            )
+
+    loop(seqs, pack_copies)
+
     gout_copy = remote(
         gout_ref, gout_buf.at[side], gout_send.at[0], gout_recv.at[0], me_s, partner
     )
     gout_copy.start()
-    gout_buf[side] = gout_ref[...]
 
     def row_part(offset):
         q = quarter
@@ -296,6 +305,7 @@
 
     loop(pairs, attn_copies)
 
+    own_inputs[3].wait()
     gout_copy.wait_recv()
 
     def rest(step):
@@ -386,12 +396,8 @@
 
 def write_kernel(*refs):
     count = len(refs) // 2
-    sems = refs[-1]
-    copies = [pltpu.make_async_copy(refs[i], refs[count + i], sems.at[i]) for i in range(count)]
-    for copy in copies:
-        copy.start()
-    for copy in copies:
-        copy.wait()
+    for i in range(count):
+        refs[count + i][...] = refs[i][...]
 
 
 def local(queries, keys, values, local_span, wo_local, wo_strided, grad_out):
@@ -412,9 +418,10 @@
             jax.ShapeDtypeStruct((HALF, rows), f32),
             jax.ShapeDtypeStruct((HALF, rows), f32),
         ),
-        in_specs=[pl.BlockSpec(memory_space=pltpu.SMEM), vmem, vmem, vmem, vmem, hbm, hbm],
+        in_specs=[pl.BlockSpec(memory_space=pltpu.SMEM)] + [hbm] * 6,
         out_specs=(vmem, vmem, vmem, vmem),
         scratch_shapes=[
+            pltpu.VMEM((3, HALF, rows), f32),
             pltpu.VMEM((heads, share, HALF // share, 2 * width), f32),
             pltpu.VMEM((seqs, RUNS + 1, res, HDIM), f32),
             pltpu.VMEM((2, seqs, RUNS + 1, res, HDIM), f32),
@@ -431,6 +438,7 @@
             pltpu.VMEM((rows, width), f32),
             pltpu.VMEM((2, seqs, RUNS + 1, res, HDIM), f32),
             pltpu.VMEM((2, seqs, RUNS + 1, res, HDIM), f32),
+            dma((4,)),
             dma((1,)),
             dma((pairs, share)),
             dma((max(1, share.bit_length() - 1),)),
@@ -448,7 +456,7 @@
             dma((1,)),
         ],
         compiler_params=pltpu.CompilerParams(
-            collective_id=0, has_side_effects=True, vmem_limit_bytes=48 * 1024 * 1024
+            collective_id=0, has_side_effects=True, vmem_limit_bytes=60 * 1024 * 1024
         ),
         cost_estimate=pl.CostEstimate(
             flops=2 * rows * 2 * width * HDIM * pairs * 5,
@@ -456,13 +464,12 @@
             transcendentals=rows * rows,
         ),
     )(local_span, queries.T, keys.T, values.T, grad_out, wo_local, wo_strided)
-    anywhere = pl.BlockSpec(memory_space=pl.ANY)
     mixed, grad_queries, grad_keys, grad_values = pl.pallas_call(
         write_kernel,
         out_shape=[jax.ShapeDtypeStruct(x.shape, x.dtype) for x in results],
-        in_specs=[anywhere] * len(results),
-        out_specs=[hbm] * len(results),
-        scratch_shapes=[dma((len(results),))],
+        in_specs=[vmem] * len(results),
+        out_specs=[vmem] * len(results),
+        compiler_params=pltpu.CompilerParams(vmem_limit_bytes=60 * 1024 * 1024),
     )(*results)
     return (mixed, grad_queries.T, grad_keys.T, grad_values.T)
 

time: 90.7 us -> 60 us (0.66)
  Pallas kernels: 80.3 us -> 59.1 us
  local copies, waits for them, and re-layouts: 9.24 us -> 0 us
    pallas_call x1, Pallas kernels: 23 us -> 1.95 us  [local(): pl.pallas_call(write_kernel, out_shape=[jax.ShapeDtypeStruct(x.shape, x.d...]
    unnamed x22 -> x0, local copies, waits for them, and re-layouts: 9.24 us -> none
where the time goes in v5:
time: 60 us; the launch traced here: 59.8 us
  Pallas kernels  59.1 us (98%)
  between operations  0.64 us (1%)
    pallas_call x1, Pallas kernels, local(): pl.pallas_call(functools.partial(kernel, seqs, heads, share), out_shape=(...  57.2 us
    pallas_call x1, Pallas kernels, local(): pl.pallas_call(write_kernel, out_shape=[jax.ShapeDtypeStruct(x.shape, x.d...  1.95 us

profile of v5, /device:TPU:1, one launch (start us, length us, event | category | flops | bytes accessed | tf_op | source)
XLA Modules:
  0.0 59.8 jit_solution(11862489353023049115)
XLA Ops:
  0.6 57.2 %shard_map.102 = (f32[256,512]{1,0:T(8,128)}, f32[64,256]{1,0:T(8,128)}, f32[64,256]{1,0:T(8,128)}, f32[64,256]{1,0:T(8,128)}) custom-call(s32[4]{0:T(128)} %span_ref.1, f32[64,256]{1,0:T(8,128)} %bitcast.6, f32[64,256]{1,0:T(8,128)} %bitcast.7, f32[64,256]{1,0:T(8,128)} %bitcast.8, bf16[256,512]{1,0:T(8,128)(2,1)} %gout_ref.1, f32[64,4096]{1,0:T(8,128)} %wo_local_ref.1, ...), custom_call_target="tpu_custom_call" | custom-call | flops 1342177280 | bytes 2097152 | tf_op jit(solution)/shard_map/pallas_call | solution.py:413
  57.8 1.9 %shard_map.103 = (f32[256,512]{1,0:T(8,128)}, f32[64,256]{1,0:T(8,128)}, f32[64,256]{1,0:T(8,128)}, f32[64,256]{1,0:T(8,128)}) custom-call(f32[256,512]{1,0:T(8,128)} %get-tuple-element.12.refs_0_, f32[64,256]{1,0:T(8,128)} %get-tuple-element.13.refs_1_, f32[64,256]{1,0:T(8,128)} %get-tuple-element.14.refs_2_, f32[64,256]{1,0:T(8,128)} %get-tuple-element.15.refs_3_), custom_call_target="tpu_custom_call" | custom-call | tf_op jit(solution)/shard_map/pallas_call | solution.py:467

commit v6 on v5

--- a/solution.py
+++ b/solution.py
@@ -219,14 +219,10 @@
     def partial_grad(g):
         for offset in fresh:
             w_arrived(g, offset)
-        w_high, w_low = halves(head_rows(g))
-        total = jnp.zeros((rows, HDIM), jnp.float32)
-        for c in range(2):
-            cols = slice(c * width, (c + 1) * width)
-            out = gout_buf[c]
-            total = total + (
-                bf16_dot(out, w_high[:, cols], NT) + bf16_dot(out, w_low[:, cols], NT)
-            )
+        w_both = jnp.concatenate(halves(head_rows(g)), axis=0)
+        total = bf16_dot(gout_buf[0], w_both[:, :width], NT)
+        total = total + bf16_dot(gout_buf[1], w_both[:, width:], NT)
+        total = total[:, :HDIM] + total[:, HDIM:]
         for a in range(RUNS):
             gpart[g, :, a] = total[a * STRIDE : (a + 1) * STRIDE].reshape(seqs, res, HDIM)
         g_copies(g)
@@ -313,26 +309,30 @@
 
     loop(pairs + len(stages) - ahead, rest)
 
-    m_buf[...] = jnp.zeros_like(m_buf)
-
-    def partial_mixed(step):
-        g = exclusive(step, pair)
-        arrived(attn_buf.at[g], attn_recv.at[g])
-        attn = jnp.concatenate(
-            [attn_buf[g, :, a].reshape(STRIDE, HDIM) for a in range(RUNS)], axis=0
-        )
-        a_high, a_low = halves(attn)
-        w_high, w_low = halves(head_rows(g))
-        for c in range(2):
-            cols = slice(c * width, (c + 1) * width)
-            m_buf[c] += bf16_dot(a_high, w_high[:, cols], NN) + (
-                bf16_dot(a_high, w_low[:, cols], NN) + bf16_dot(a_low, w_high[:, cols], NN)
-            )
-
-    loop(pairs, partial_mixed)
-    m_copy = remote(
-        m_buf.at[1 - side], m_recv, m_send.at[0], m_recv_sem.at[0], me_s, partner
-    )
+    def partial_mixed(half, at, wait):
+        def body(i):
+            attn_parts, w_parts = [], []
+            for n in range(2):
+                g = exclusive(2 * i + n, pair)
+                if wait:
+                    arrived(attn_buf.at[g], attn_recv.at[g])
+                attn = jnp.concatenate(
+                    [attn_buf[g, :, a].reshape(STRIDE, HDIM) for a in range(RUNS)], axis=0
+                )
+                both = head_rows(g)
+                a_high, a_low = halves(attn)
+                w_high, w_low = halves(jnp.where(half == 0, both[:, :width], both[:, width:]))
+                attn_parts += [a_high, a_low, a_high]
+                w_parts += [w_high, w_high, w_low]
+            m_buf[at] += bf16_dot(
+                jnp.concatenate(attn_parts, axis=1), jnp.concatenate(w_parts, axis=0), NN
+            )
+
+        m_buf[at] = jnp.zeros((rows, width), jnp.float32)
+        loop(pairs // 2, body)
+
+    partial_mixed(1 - side, 0, True)
+    m_copy = remote(m_buf.at[0], m_recv, m_send.at[0], m_recv_sem.at[0], me_s, partner)
     m_copy.start()
 
     arrived(g_buf, g_recv.at[0])
@@ -360,6 +360,8 @@
 
     loop(seqs, e_copies)
 
+    partial_mixed(side, 1, False)
+
     arrived(pack_ref, pack_send.at[1 - side])
     arrived(w_buf.at[pl.ds(0, heads - 1), 0], w_send.at[0])
     gout_copy.wait_send()
@@ -375,7 +377,7 @@
         arrived(attn_own.at[pl.ds(0, seqs - 1)], g_send.at[1])
 
     m_copy.wait_recv()
-    mixed_ref[...] = m_buf[side] + m_recv[...]
+    mixed_ref[...] = m_buf[1] + m_recv[...]
 
     arrived(e_buf, e_recv.at[0])
     grads = e_buf[0] + e_buf[1]

time: 60 us -> 58.4 us (0.973)
  Pallas kernels: 59.1 us -> 57.6 us
    pallas_call x1, Pallas kernels: 57.2 us -> 55.7 us  [local(): pl.pallas_call(functools.partial(kernel, seqs, heads, share), out_shape=(...]
where the time goes in v6:
time: 58.4 us; the launch traced here: 58.3 us
  Pallas kernels  57.6 us (99%)
  between operations  0.64 us (1%)
    pallas_call x1, Pallas kernels, local(): pl.pallas_call(functools.partial(kernel, seqs, heads, share), out_shape=(...  55.7 us
    pallas_call x1, Pallas kernels, local(): pl.pallas_call(write_kernel, out_shape=[jax.ShapeDtypeStruct(x.shape, x.d...  1.95 us

profile of v6, /device:TPU:1, one launch (start us, length us, event | category | flops | bytes accessed | tf_op | source)
XLA Modules:
  0.0 58.3 jit_solution(4305724629964525226)
XLA Ops:
  0.6 55.7 %shard_map.102 = (f32[256,512]{1,0:T(8,128)}, f32[64,256]{1,0:T(8,128)}, f32[64,256]{1,0:T(8,128)}, f32[64,256]{1,0:T(8,128)}) custom-call(s32[4]{0:T(128)} %span_ref.1, f32[64,256]{1,0:T(8,128)} %bitcast.6, f32[64,256]{1,0:T(8,128)} %bitcast.7, f32[64,256]{1,0:T(8,128)} %bitcast.8, bf16[256,512]{1,0:T(8,128)(2,1)} %gout_ref.1, f32[64,4096]{1,0:T(8,128)} %wo_local_ref.1, ...), custom_call_target="tpu_custom_call" | custom-call | flops 1342177280 | bytes 2097152 | tf_op jit(solution)/shard_map/pallas_call | solution.py:415
  56.3 1.9 %shard_map.103 = (f32[256,512]{1,0:T(8,128)}, f32[64,256]{1,0:T(8,128)}, f32[64,256]{1,0:T(8,128)}, f32[64,256]{1,0:T(8,128)}) custom-call(f32[256,512]{1,0:T(8,128)} %get-tuple-element.12.refs_0_, f32[64,256]{1,0:T(8,128)} %get-tuple-element.13.refs_1_, f32[64,256]{1,0:T(8,128)} %get-tuple-element.14.refs_2_, f32[64,256]{1,0:T(8,128)} %get-tuple-element.15.refs_3_), custom_call_target="tpu_custom_call" | custom-call | tf_op jit(solution)/shard_map/pallas_call | solution.py:469

commit v7 on v6

--- a/solution.py
+++ b/solution.py
@@ -216,7 +216,12 @@
 
         loop(seqs, one)
 
-    def partial_grad(g):
+    def partial_grad(turn_of, g):
+        @pl.when(turn_of == 0)
+        def _():
+            own_inputs[3].wait()
+            gout_copy.wait_recv()
+
         for offset in fresh:
             w_arrived(g, offset)
         w_both = jnp.concatenate(halves(head_rows(g)), axis=0)
@@ -237,7 +242,7 @@
                 if at < len(stages):
                     run_stage(at, z)
                 else:
-                    partial_grad(z)
+                    partial_grad(turn_of, z)
 
     ahead = 2
 
@@ -300,9 +305,6 @@
         loop(seqs, one)
 
     loop(pairs, attn_copies)
-
-    own_inputs[3].wait()
-    gout_copy.wait_recv()
 
     def rest(step):
         w_step(step + ahead + 1)

time: 58.4 us -> 58.5 us (level)
  no operation moved by 1% of the time
where the time goes in v7:
time: 58.5 us; the launch traced here: 58.3 us
  Pallas kernels  57.7 us (99%)
  between operations  0.64 us (1%)
    pallas_call x1, Pallas kernels, local(): pl.pallas_call(functools.partial(kernel, seqs, heads, share), out_shape=(...  55.7 us
    pallas_call x1, Pallas kernels, local(): pl.pallas_call(write_kernel, out_shape=[jax.ShapeDtypeStruct(x.shape, x.d...  1.95 us

profile of v7, /device:TPU:1, one launch (start us, length us, event | category | flops | bytes accessed | tf_op | source)
XLA Modules:
  0.0 58.3 jit_solution(4937116200483535034)
XLA Ops:
  0.6 55.7 %shard_map.102 = (f32[256,512]{1,0:T(8,128)}, f32[64,256]{1,0:T(8,128)}, f32[64,256]{1,0:T(8,128)}, f32[64,256]{1,0:T(8,128)}) custom-call(s32[4]{0:T(128)} %span_ref.1, f32[64,256]{1,0:T(8,128)} %bitcast.6, f32[64,256]{1,0:T(8,128)} %bitcast.7, f32[64,256]{1,0:T(8,128)} %bitcast.8, bf16[256,512]{1,0:T(8,128)(2,1)} %gout_ref.1, f32[64,4096]{1,0:T(8,128)} %wo_local_ref.1, ...), custom_call_target="tpu_custom_call" | custom-call | flops 1342177280 | bytes 2097152 | tf_op jit(solution)/shard_map/pallas_call | solution.py:417
  56.3 1.9 %shard_map.103 = (f32[256,512]{1,0:T(8,128)}, f32[64,256]{1,0:T(8,128)}, f32[64,256]{1,0:T(8,128)}, f32[64,256]{1,0:T(8,128)}) custom-call(f32[256,512]{1,0:T(8,128)} %get-tuple-element.12.refs_0_, f32[64,256]{1,0:T(8,128)} %get-tuple-element.13.refs_1_, f32[64,256]{1,0:T(8,128)} %get-tuple-element.14.refs_2_, f32[64,256]{1,0:T(8,128)} %get-tuple-element.15.refs_3_), custom_call_target="tpu_custom_call" | custom-call | tf_op jit(solution)/shard_map/pallas_call | solution.py:471

commit v8 on v7

--- a/solution.py
+++ b/solution.py
@@ -289,7 +289,6 @@
     weights = jnp.where(allowed, jnp.exp(scores - row_max), 0.0)
     probs = weights / jnp.sum(weights, axis=-1, keepdims=True)
     p_buf[...] = probs
-    w_step(ahead)
     attended = exact_dot(probs, v_buf[...].reshape(rows, HDIM), NN)
     attn_own[...] = attended.reshape(seqs, RUNS, res, HDIM)
 
@@ -305,6 +304,7 @@
         loop(seqs, one)
 
     loop(pairs, attn_copies)
+    w_step(ahead)
 
     def rest(step):
         w_step(step + ahead + 1)

time: 58.5 us -> 59.1 us (1.010)
  Pallas kernels: 57.7 us -> 58.3 us
    pallas_call x1, Pallas kernels: 55.7 us -> 56.4 us  [local(): pl.pallas_call(functools.partial(kernel, seqs, heads, share), out_shape=(...]
where the time goes in v8:
time: 59.1 us; the launch traced here: 59 us
  Pallas kernels  58.3 us (99%)
  between operations  0.64 us (1%)
    pallas_call x1, Pallas kernels, local(): pl.pallas_call(functools.partial(kernel, seqs, heads, share), out_shape=(...  56.4 us
    pallas_call x1, Pallas kernels, local(): pl.pallas_call(write_kernel, out_shape=[jax.ShapeDtypeStruct(x.shape, x.d...  1.95 us

profile of v8, /device:TPU:1, one launch (start us, length us, event | category | flops | bytes accessed | tf_op | source)
XLA Modules:
  0.0 59.0 jit_solution(7431872455615889676)
XLA Ops:
  0.6 56.4 %shard_map.102 = (f32[256,512]{1,0:T(8,128)}, f32[64,256]{1,0:T(8,128)}, f32[64,256]{1,0:T(8,128)}, f32[64,256]{1,0:T(8,128)}) custom-call(s32[4]{0:T(128)} %span_ref.1, f32[64,256]{1,0:T(8,128)} %bitcast.6, f32[64,256]{1,0:T(8,128)} %bitcast.7, f32[64,256]{1,0:T(8,128)} %bitcast.8, bf16[256,512]{1,0:T(8,128)(2,1)} %gout_ref.1, f32[64,4096]{1,0:T(8,128)} %wo_local_ref.1, ...), custom_call_target="tpu_custom_call" | custom-call | flops 1342177280 | bytes 2097152 | tf_op jit(solution)/shard_map/pallas_call | solution.py:417
  57.0 1.9 %shard_map.103 = (f32[256,512]{1,0:T(8,128)}, f32[64,256]{1,0:T(8,128)}, f32[64,256]{1,0:T(8,128)}, f32[64,256]{1,0:T(8,128)}) custom-call(f32[256,512]{1,0:T(8,128)} %get-tuple-element.12.refs_0_, f32[64,256]{1,0:T(8,128)} %get-tuple-element.13.refs_1_, f32[64,256]{1,0:T(8,128)} %get-tuple-element.14.refs_2_, f32[64,256]{1,0:T(8,128)} %get-tuple-element.15.refs_3_), custom_call_target="tpu_custom_call" | custom-call | tf_op jit(solution)/shard_map/pallas_call | solution.py:471
